TPU v7x, 32 devices: a whole 2x2x4 slice. The times are simulated.
32 devices in a mesh: dp: 8 (over y, x, core), mp: 4 (over z).
Axes of the slice: x: 2, y: 2, z: 4, core: 2. Of those that a mesh axis runs over, the one named last changes fastest.
Arguments:
- patches: bfloat16 [12288, 768], P(('dp', 'mp')), may hold values from -6 to 6
- cotangent: bfloat16 [12288, 768], P(('dp', 'mp')), may hold values from -6 to 6
- conditioning: bfloat16 [24, 768], P('dp'), may hold values from -6 to 6
- lengths: int32 [8, 3], P('dp'), may hold values from 1 to 768, 1536 in all within a row
- routes: int32 [12288, 2], P('dp'), may hold values from 0 to 7, all different within a row; in each aligned block of 1536 rows (0 to 1535, 1536 to 3071, ...) at most 480 rows name the same one
- ada_weight: float32 [768, 4608], P(None, ('dp', 'mp')), may hold values from -0.21875 to 0.21875
- ada_first: float32 [768, 4608], P(None, ('dp', 'mp')), may hold values from -32 to 32
- ada_second: float32 [768, 4608], P(None, ('dp', 'mp')), may hold values from 81.1008 to 1290.24
- router_weight: float32 [6144], P(('dp', 'mp')), may hold values from -0.15625 to 0.15625
- router_first: float32 [6144], P(('dp', 'mp')), may hold values from -32 to 32
- router_second: float32 [6144], P(('dp', 'mp')), may hold values from 81.1008 to 1290.24
- qkv_weight: float32 [768, 2304], P('dp', 'mp'), may hold values from -0.21875 to 0.21875
- qkv_first: float32 [768, 2304], P('dp', 'mp'), may hold values from -20 to 20
- qkv_second: float32 [768, 2304], P('dp', 'mp'), may hold values from 29.4912 to 466.944
- proj_weight: float32 [768, 768], P('mp', 'dp'), may hold values from -1.5 to 1.5
- proj_first: float32 [768, 768], P('mp', 'dp'), may hold values from -32 to 32
- proj_second: float32 [768, 768], P('mp', 'dp'), may hold values from 61.44 to 983.04
- shared_in_weight: float32 [768, 3072], P('dp', 'mp'), may hold values from -0.21875 to 0.21875
- shared_in_first: float32 [768, 3072], P('dp', 'mp'), may hold values from -28 to 28
- shared_in_second: float32 [768, 3072], P('dp', 'mp'), may hold values from 51.6096 to 823.296
- shared_out_weight: float32 [3072, 768], P('mp', 'dp'), may hold values from -0.109375 to 0.109375
- shared_out_first: float32 [3072, 768], P('mp', 'dp'), may hold values from -28 to 28
- shared_out_second: float32 [3072, 768], P('mp', 'dp'), may hold values from 51.6096 to 823.296
- expert_in_weight: float32 [8, 768, 3072], P(None, 'dp', 'mp'), may hold values from -0.21875 to 0.21875
- expert_in_first: float32 [8, 768, 3072], P(None, 'dp', 'mp'), may hold values from -7 to 7
- expert_in_second: float32 [8, 768, 3072], P(None, 'dp', 'mp'), may hold values from 3.19488 to 51.6096
- expert_out_weight: float32 [8, 3072, 768], P(None, 'mp', 'dp'), may hold values from -0.109375 to 0.109375
- expert_out_first: float32 [8, 3072, 768], P(None, 'mp', 'dp'), may hold values from -7 to 7
- expert_out_second: float32 [8, 3072, 768], P(None, 'mp', 'dp'), may hold values from 3.19488 to 51.6096
Outputs:
- result: bfloat16 [12288, 768], P(('dp', 'mp'))
- patch_grad: bfloat16 [12288, 768], P(('dp', 'mp'))
- ada_weight_new: float32 [768, 4608], P(None, ('dp', 'mp'))
- ada_first_new: float32 [768, 4608], P(None, ('dp', 'mp'))
- ada_second_new: float32 [768, 4608], P(None, ('dp', 'mp'))
- ada_weight_low: bfloat16 [768, 4608], P(None, ('dp', 'mp'))
- router_weight_new: float32 [6144], P(('dp', 'mp'))
- router_first_new: float32 [6144], P(('dp', 'mp'))
- router_second_new: float32 [6144], P(('dp', 'mp'))
- router_weight_low: bfloat16 [6144], P(('dp', 'mp'))
- qkv_weight_new: float32 [768, 2304], P('dp', 'mp')
- qkv_first_new: float32 [768, 2304], P('dp', 'mp')
- qkv_second_new: float32 [768, 2304], P('dp', 'mp')
- qkv_weight_low: bfloat16 [768, 2304], P('dp', 'mp')
- proj_weight_new: float32 [768, 768], P('mp', 'dp')
- proj_first_new: float32 [768, 768], P('mp', 'dp')
- proj_second_new: float32 [768, 768], P('mp', 'dp')
- proj_weight_low: bfloat16 [768, 768], P('mp', 'dp')
- shared_in_weight_new: float32 [768, 3072], P('dp', 'mp')
- shared_in_first_new: float32 [768, 3072], P('dp', 'mp')
- shared_in_second_new: float32 [768, 3072], P('dp', 'mp')
- shared_in_weight_low: bfloat16 [768, 3072], P('dp', 'mp')
- shared_out_weight_new: float32 [3072, 768], P('mp', 'dp')
- shared_out_first_new: float32 [3072, 768], P('mp', 'dp')
- shared_out_second_new: float32 [3072, 768], P('mp', 'dp')
- shared_out_weight_low: bfloat16 [3072, 768], P('mp', 'dp')
- expert_in_weight_new: float32 [8, 768, 3072], P(None, 'dp', 'mp')
- expert_in_first_new: float32 [8, 768, 3072], P(None, 'dp', 'mp')
- expert_in_second_new: float32 [8, 768, 3072], P(None, 'dp', 'mp')
- expert_in_weight_low: bfloat16 [8, 768, 3072], P(None, 'dp', 'mp')
- expert_out_weight_new: float32 [8, 3072, 768], P(None, 'mp', 'dp')
- expert_out_first_new: float32 [8, 3072, 768], P(None, 'mp', 'dp')
- expert_out_second_new: float32 [8, 3072, 768], P(None, 'mp', 'dp')
- expert_out_weight_low: bfloat16 [8, 3072, 768], P(None, 'mp', 'dp')
Inputs may be any that keep to these rules, and one draw needn't show every extreme that they name: Each group's 3 lengths add up to 1536; the largest is exactly 768. `routes`: A row names two different experts; within each group's 1536 rows no expert is named by more than 480 rows, a bound that some block reaches.
All inputs are finite; a program needn't handle non-finite values.
Results may differ from a plain program's by a relative error of at most 0.033.
The roundings to bfloat16 on the way count: a program that leaves them out, or rounds other values in their place, can miss the bound.
Values may be sent and summed in bfloat16 or wider, within the bound.
No kernel may reach another device: no remote copies, remote signals or barrier semaphores. Data moves between devices by JAX's collectives and lax.ppermute only.
A program may use at most 256 MiB of HBM per device.

v0:
```python
import jax
import jax.numpy as jnp
from jax import lax
from jax.sharding import PartitionSpec as P

D = 768
H = 12
HD = 64
FF = 3072
E = 8
STEP = 10


beta_one = 0.9
beta_two = 0.95
epsilon = 1e-08
weight_decay = 0.1
norm_floor = 1e-06
highest = lax.Precision.HIGHEST


def layer_norm(values):
    centred = values - jnp.mean(values, axis=1, keepdims=True)
    spread = jnp.mean(centred * centred, axis=1, keepdims=True)
    return centred * lax.rsqrt(spread + norm_floor)


def modulate(values, shift_term, scaling):
    return layer_norm(values) * (1.0 + scaling) + shift_term


def gelu_back(before, gradient):
    return jax.vjp(jax.nn.gelu, before)[1](gradient)[0]


def slot_tables(route_ids, capacity):
    flattened = route_ids.reshape(-1)
    markers = (flattened[:, None] == jnp.arange(E, dtype=jnp.int32)[None, :]).astype(jnp.int32)
    earlier = jnp.cumsum(markers, axis=0) - markers
    positions = jnp.sum(earlier * markers, axis=1)
    destination = flattened * capacity + positions
    owner_rows = jnp.arange(flattened.shape[0], dtype=jnp.int32) // 2
    slot_token = jnp.zeros((E * capacity,), jnp.int32).at[destination].set(owner_rows)
    occupied = jnp.zeros((E * capacity,), jnp.int32).at[destination].set(1)
    return (destination.reshape(-1, 2), slot_token, occupied)


def adamw_update(master, first, second, gradient, fan_in):
    step_rate = 0.5 * fan_in ** (-0.5)
    first_new = beta_one * first + (1.0 - beta_one) * gradient
    second_new = beta_two * second + (1.0 - beta_two) * gradient * gradient
    first_hat = first_new / (1.0 - beta_one**STEP)
    second_hat = second_new / (1.0 - beta_two**STEP)
    master_new = master - step_rate * (
        first_hat / (jnp.sqrt(second_hat) + epsilon) + weight_decay * master
    )
    return (master_new, first_new, second_new, master_new.astype(jnp.bfloat16))


def body(
    patches,
    cotangent,
    conditioning,
    lengths,
    routes,
    ada_weight,
    ada_first,
    ada_second,
    router_weight,
    router_first,
    router_second,
    qkv_weight,
    qkv_first,
    qkv_second,
    proj_weight,
    proj_first,
    proj_second,
    shared_in_weight,
    shared_in_first,
    shared_in_second,
    shared_out_weight,
    shared_out_first,
    shared_out_second,
    expert_in_weight,
    expert_in_first,
    expert_in_second,
    expert_out_weight,
    expert_out_first,
    expert_out_second,
):
    tok_rows = patches.shape[0]
    width = lax.axis_size("mp")
    group = tok_rows * width
    capacity = 5 * group // 16
    heads_here = H // width
    qrows = 512
    block_count = group // qrows
    scaling = HD ** (-0.5)
    model_rank = lax.axis_index("mp")
    data_rank = lax.axis_index("dp")
    item_count = lengths.shape[1]
    ada_full, router_full = (
        lax.all_gather(ada_weight.astype(jnp.bfloat16), ("dp", "mp"), axis=1, tiled=True),
        lax.all_gather(router_weight.astype(jnp.bfloat16), ("dp", "mp"), axis=0, tiled=True),
    )
    router_matrix = router_full.reshape(D, E)
    (
        qkv_here,
        proj_here,
        shared_in_here,
        shared_out_here,
        expert_in_here,
        expert_out_here,
        cond_all,
    ) = (
        lax.all_gather(qkv_weight.astype(jnp.bfloat16), "dp", axis=0, tiled=True),
        lax.all_gather(proj_weight.astype(jnp.bfloat16), "dp", axis=1, tiled=True),
        lax.all_gather(shared_in_weight.astype(jnp.bfloat16), "dp", axis=0, tiled=True),
        lax.all_gather(shared_out_weight.astype(jnp.bfloat16), "dp", axis=1, tiled=True),
        lax.all_gather(expert_in_weight.astype(jnp.bfloat16), "dp", axis=1, tiled=True),
        lax.all_gather(expert_out_weight.astype(jnp.bfloat16), "dp", axis=2, tiled=True),
        lax.all_gather(conditioning, "dp", axis=0, tiled=True),
    )
    cond_mine = lax.dynamic_slice_in_dim(cond_all, data_rank * item_count, item_count, 0)
    bounds = jnp.cumsum(lengths[0])
    positions = jnp.arange(group, dtype=jnp.int32)
    segment = jnp.sum((positions[:, None] >= bounds[None, :]).astype(jnp.int32), axis=1)
    item_marks = (segment[:, None] == jnp.arange(item_count, dtype=jnp.int32)[None, :]).astype(
        jnp.float32
    )
    mine_marks = lax.dynamic_slice_in_dim(item_marks, model_rank * tok_rows, tok_rows, 0)
    cond_act = jax.nn.silu(cond_mine.astype(jnp.float32)).astype(jnp.bfloat16)
    modulation = jnp.dot(cond_act, ada_full, preferred_element_type=jnp.float32)
    token_mod = jnp.dot(mine_marks, modulation, precision=highest)
    shift_one, scale_one, gate_one, shift_two, scale_two, gate_two = jnp.split(token_mod, 6, axis=1)
    states = patches.astype(jnp.float32)
    h_one = modulate(states, shift_one, scale_one).astype(jnp.bfloat16)
    h_one_all = lax.all_gather(h_one, "mp", axis=0, tiled=True)
    qkv = jnp.dot(h_one_all, qkv_here, preferred_element_type=jnp.float32).astype(jnp.bfloat16)
    qkv = qkv.reshape(group, heads_here, 3, HD)
    queries = qkv[:, :, 0]
    key_rows = qkv[:, :, 1]
    value_rows = qkv[:, :, 2]
    starts = jnp.arange(block_count, dtype=jnp.int32) * qrows

    def block_scores(row_start):
        query_rows = lax.dynamic_slice_in_dim(queries, row_start, qrows, 0)
        query_items = lax.dynamic_slice_in_dim(segment, row_start, qrows, 0)
        scores = (
            jnp.einsum("qhd,khd->hqk", query_rows, key_rows, preferred_element_type=jnp.float32)
            * scaling
        )
        allowed = query_items[:, None] == segment[None, :]
        return (query_rows, jnp.where(allowed[None], scores, -1e30))

    def attend_block(row_start):
        query_rows, scores = block_scores(row_start)
        row_peak = jnp.max(scores, axis=2, keepdims=True)
        exps = jnp.exp(scores - row_peak)
        row_total = jnp.sum(exps, axis=2, keepdims=True)
        attn_probs = (exps / row_total).astype(jnp.bfloat16)
        mixed_block = jnp.einsum(
            "hqk,khd->qhd", attn_probs, value_rows, preferred_element_type=jnp.float32
        )
        return (mixed_block.astype(jnp.bfloat16), (row_peak + jnp.log(row_total))[:, :, 0])

    mixed_blocks, log_totals = lax.map(attend_block, starts)
    mixed_rows = mixed_blocks.reshape(group, heads_here * HD)
    attn_branch = lax.psum_scatter(
        jnp.dot(mixed_rows, proj_here, preferred_element_type=jnp.float32),
        "mp",
        scatter_dimension=0,
        tiled=True,
    )
    x_one = states + gate_one * attn_branch
    h_two = modulate(x_one, shift_two, scale_two).astype(jnp.bfloat16)
    h_two_all = lax.all_gather(h_two, "mp", axis=0, tiled=True)
    shared_pre = jnp.dot(h_two_all, shared_in_here, preferred_element_type=jnp.float32)
    shared_act = jax.nn.gelu(shared_pre).astype(jnp.bfloat16)
    shared_res = jnp.dot(shared_act, shared_out_here, preferred_element_type=jnp.float32)
    logits = jnp.dot(h_two_all, router_matrix, preferred_element_type=jnp.float32)
    markers = (routes[:, :, None] == jnp.arange(E, dtype=jnp.int32)[None, None, :]).astype(
        jnp.float32
    )
    picked = jnp.sum(markers * logits[:, None, :], axis=2)
    gates = jax.nn.softmax(picked, axis=1)
    destination, slot_token, occupied = slot_tables(routes, capacity)
    dispatched = jnp.where(
        occupied[:, None] > 0, h_two_all[slot_token], jnp.zeros((), jnp.bfloat16)
    ).reshape(E, capacity, D)
    expert_pre = jnp.einsum(
        "ecd,edf->ecf", dispatched, expert_in_here, preferred_element_type=jnp.float32
    )
    expert_act = jax.nn.gelu(expert_pre).astype(jnp.bfloat16)
    expert_res = jnp.einsum(
        "ecf,efd->ecd", expert_act, expert_out_here, preferred_element_type=jnp.float32
    ).reshape(E * capacity, D)
    first_res = expert_res[destination[:, 0]]
    second_res = expert_res[destination[:, 1]]
    mixture = gates[:, 0:1] * first_res + gates[:, 1:2] * second_res
    mlp_branch = lax.psum_scatter(
        (shared_res + mixture).astype(jnp.bfloat16), "mp", scatter_dimension=0, tiled=True
    ).astype(jnp.float32)
    outcome = x_one + gate_two * mlp_branch
    grad_out = cotangent.astype(jnp.float32)
    grad_gate_two = grad_out * mlp_branch
    grad_branch = (gate_two * grad_out).astype(jnp.bfloat16)
    grad_branch_all = lax.all_gather(grad_branch, "mp", axis=0, tiled=True)
    grad_shared_out = jnp.einsum(
        "gf,gd->fd", shared_act, grad_branch_all, preferred_element_type=jnp.float32
    )
    grad_shared_act = jnp.einsum(
        "gd,fd->gf", grad_branch_all, shared_out_here, preferred_element_type=jnp.float32
    )
    grad_shared_pre = gelu_back(shared_pre, grad_shared_act).astype(jnp.bfloat16)
    grad_shared_in = jnp.einsum(
        "gd,gf->df", h_two_all, grad_shared_pre, preferred_element_type=jnp.float32
    )
    grad_h_two = jnp.einsum(
        "gf,df->gd", grad_shared_pre, shared_in_here, preferred_element_type=jnp.float32
    )
    gate_slot = (
        jnp.zeros((E * capacity,), jnp.float32).at[destination.reshape(-1)].set(gates.reshape(-1))
    )
    grad_res = (
        (gate_slot[:, None] * grad_branch_all[slot_token].astype(jnp.float32))
        .astype(jnp.bfloat16)
        .reshape(E, capacity, D)
    )
    grad_expert_out = jnp.einsum(
        "ecf,ecd->efd", expert_act, grad_res, preferred_element_type=jnp.float32
    )
    grad_expert_act = jnp.einsum(
        "ecd,efd->ecf", grad_res, expert_out_here, preferred_element_type=jnp.float32
    )
    grad_expert_pre = gelu_back(expert_pre, grad_expert_act).astype(jnp.bfloat16)
    grad_expert_in = jnp.einsum(
        "ecd,ecf->edf", dispatched, grad_expert_pre, preferred_element_type=jnp.float32
    )
    grad_dispatched = jnp.einsum(
        "ecf,edf->ecd", grad_expert_pre, expert_in_here, preferred_element_type=jnp.float32
    ).reshape(E * capacity, D)
    grad_h_two = (
        grad_h_two + grad_dispatched[destination[:, 0]] + grad_dispatched[destination[:, 1]]
    )
    branch_wide = grad_branch_all.astype(jnp.float32)
    grad_gates = jnp.stack(
        [jnp.sum(branch_wide * first_res, axis=1), jnp.sum(branch_wide * second_res, axis=1)],
        axis=1,
    )
    grad_picked = gates * (grad_gates - jnp.sum(gates * grad_gates, axis=1, keepdims=True))
    grad_logits = jnp.sum(markers * grad_picked[:, :, None], axis=1)
    grad_router = jnp.einsum(
        "gd,ge->de", h_two_all.astype(jnp.float32), grad_logits, precision=highest
    )
    grad_h_two = grad_h_two + jnp.einsum(
        "ge,de->gd", grad_logits, router_matrix.astype(jnp.float32), precision=highest
    )
    grad_h_two_mine = lax.psum_scatter(
        grad_h_two.astype(jnp.bfloat16), "mp", scatter_dimension=0, tiled=True
    ).astype(jnp.float32)
    pull_two = jax.vjp(modulate, x_one, shift_two, scale_two)[1]
    grad_x_one, grad_shift_two, grad_scale_two = pull_two(grad_h_two_mine)
    grad_x_one = grad_x_one + grad_out
    grad_gate_one = grad_x_one * attn_branch
    grad_attn = (gate_one * grad_x_one).astype(jnp.bfloat16)
    grad_attn_all = lax.all_gather(grad_attn, "mp", axis=0, tiled=True)
    grad_proj = jnp.einsum(
        "gc,gd->cd", mixed_rows, grad_attn_all, preferred_element_type=jnp.float32
    )
    grad_mixed = jnp.einsum(
        "gd,cd->gc", grad_attn_all, proj_here, preferred_element_type=jnp.float32
    )
    grad_mixed = grad_mixed.astype(jnp.bfloat16).reshape(group, heads_here, HD)

    def attend_back(carry, inputs):
        grad_keys, grad_values = carry
        row_start, log_block = inputs
        query_rows, scores = block_scores(row_start)
        grad_rows = lax.dynamic_slice_in_dim(grad_mixed, row_start, qrows, 0)
        soft_rows = jnp.exp(scores - log_block[:, :, None])
        soft_low = soft_rows.astype(jnp.bfloat16)
        grad_values = grad_values + jnp.einsum(
            "hqk,qhd->khd", soft_low, grad_rows, preferred_element_type=jnp.float32
        )
        grad_soft = jnp.einsum(
            "qhd,khd->hqk", grad_rows, value_rows, preferred_element_type=jnp.float32
        )
        middle = jnp.sum(soft_rows * grad_soft, axis=2, keepdims=True)
        grad_scores = (soft_rows * (grad_soft - middle)).astype(jnp.bfloat16)
        grad_query = (
            jnp.einsum("hqk,khd->qhd", grad_scores, key_rows, preferred_element_type=jnp.float32)
            * scaling
        )
        grad_keys = (
            grad_keys
            + jnp.einsum(
                "hqk,qhd->khd", grad_scores, query_rows, preferred_element_type=jnp.float32
            )
            * scaling
        )
        return ((grad_keys, grad_values), grad_query)

    zero_rows = jnp.zeros((group, heads_here, HD), jnp.float32)
    (grad_keys, grad_values), grad_queries = lax.scan(
        attend_back, (zero_rows, zero_rows), (starts, log_totals)
    )
    grad_queries = grad_queries.reshape(group, heads_here, HD)
    grad_qkv = (
        jnp.stack([grad_queries, grad_keys, grad_values], axis=2)
        .astype(jnp.bfloat16)
        .reshape(group, heads_here * 3 * HD)
    )
    grad_qkv_weight = jnp.einsum(
        "gd,gc->dc", h_one_all, grad_qkv, preferred_element_type=jnp.float32
    )
    grad_h_one = lax.psum_scatter(
        jnp.einsum("gc,dc->gd", grad_qkv, qkv_here, preferred_element_type=jnp.float32).astype(
            jnp.bfloat16
        ),
        "mp",
        scatter_dimension=0,
        tiled=True,
    ).astype(jnp.float32)
    pull_one = jax.vjp(modulate, states, shift_one, scale_one)[1]
    grad_states, grad_shift_one, grad_scale_one = pull_one(grad_h_one)
    grad_states = grad_states + grad_x_one
    grad_token_mod = jnp.concatenate(
        [
            grad_shift_one,
            grad_scale_one,
            grad_gate_one,
            grad_shift_two,
            grad_scale_two,
            grad_gate_two,
        ],
        axis=1,
    )
    grad_modulation = jnp.einsum("ti,tc->ic", mine_marks, grad_token_mod, precision=highest)
    sharded_reduced = (
        lax.psum_scatter(grad_qkv_weight, "dp", scatter_dimension=0, tiled=True),
        lax.psum_scatter(grad_proj, "dp", scatter_dimension=1, tiled=True),
        lax.psum_scatter(grad_shared_in, "dp", scatter_dimension=0, tiled=True),
        lax.psum_scatter(grad_shared_out, "dp", scatter_dimension=1, tiled=True),
        lax.psum_scatter(grad_expert_in, "dp", scatter_dimension=1, tiled=True),
        lax.psum_scatter(grad_expert_out, "dp", scatter_dimension=2, tiled=True),
    )
    grad_ada = jnp.einsum(
        "id,ic->dc", cond_act.astype(jnp.float32), grad_modulation, precision=highest
    )
    ada_grad, router_grad = (
        lax.psum_scatter(grad_ada, ("dp", "mp"), scatter_dimension=1, tiled=True),
        lax.psum_scatter(grad_router.reshape(-1), ("dp", "mp"), scatter_dimension=0, tiled=True),
    )
    gradients = (ada_grad, router_grad) + tuple(sharded_reduced)
    masters = (
        ada_weight,
        router_weight,
        qkv_weight,
        proj_weight,
        shared_in_weight,
        shared_out_weight,
        expert_in_weight,
        expert_out_weight,
    )
    firsts = (
        ada_first,
        router_first,
        qkv_first,
        proj_first,
        shared_in_first,
        shared_out_first,
        expert_in_first,
        expert_out_first,
    )
    seconds = (
        ada_second,
        router_second,
        qkv_second,
        proj_second,
        shared_in_second,
        shared_out_second,
        expert_in_second,
        expert_out_second,
    )
    fan_ins = (D, D, D, 8.0 * D / group, D, FF, D, FF)
    updates = []
    for master, first, second, gradient, fan_in in zip(
        masters, firsts, seconds, gradients, fan_ins
    ):
        updates.extend(adamw_update(master, first, second, gradient, fan_in))
    return tuple([outcome.astype(jnp.bfloat16), grad_states.astype(jnp.bfloat16)] + updates)


def solution(mesh):
    in_specs = (
        P(("dp", "mp"), None),
        P(("dp", "mp"), None),
        P("dp", None),
        P("dp", None),
        P("dp", None),
        P(None, ("dp", "mp")),
        P(None, ("dp", "mp")),
        P(None, ("dp", "mp")),
        P(("dp", "mp")),
        P(("dp", "mp")),
        P(("dp", "mp")),
        P("dp", "mp"),
        P("dp", "mp"),
        P("dp", "mp"),
        P("mp", "dp"),
        P("mp", "dp"),
        P("mp", "dp"),
        P("dp", "mp"),
        P("dp", "mp"),
        P("dp", "mp"),
        P("mp", "dp"),
        P("mp", "dp"),
        P("mp", "dp"),
        P(None, "dp", "mp"),
        P(None, "dp", "mp"),
        P(None, "dp", "mp"),
        P(None, "mp", "dp"),
        P(None, "mp", "dp"),
        P(None, "mp", "dp"),
    )
    out_specs = (
        P(("dp", "mp"), None),
        P(("dp", "mp"), None),
        P(None, ("dp", "mp")),
        P(None, ("dp", "mp")),
        P(None, ("dp", "mp")),
        P(None, ("dp", "mp")),
        P(("dp", "mp")),
        P(("dp", "mp")),
        P(("dp", "mp")),
        P(("dp", "mp")),
        P("dp", "mp"),
        P("dp", "mp"),
        P("dp", "mp"),
        P("dp", "mp"),
        P("mp", "dp"),
        P("mp", "dp"),
        P("mp", "dp"),
        P("mp", "dp"),
        P("dp", "mp"),
        P("dp", "mp"),
        P("dp", "mp"),
        P("dp", "mp"),
        P("mp", "dp"),
        P("mp", "dp"),
        P("mp", "dp"),
        P("mp", "dp"),
        P(None, "dp", "mp"),
        P(None, "dp", "mp"),
        P(None, "dp", "mp"),
        P(None, "dp", "mp"),
        P(None, "mp", "dp"),
        P(None, "mp", "dp"),
        P(None, "mp", "dp"),
        P(None, "mp", "dp"),
    )
    return jax.shard_map(body, mesh=mesh, in_specs=in_specs, out_specs=out_specs, check_vma=False)
```

profile of v0, /device:TPU:0, one launch (start us, length us, event | category | flops | bytes accessed | tf_op | source)
XLA Modules:
  0.0 1528.7 jit_solution(18270440911943098431)
XLA Ops:
  23.5 63.3 %all-gather.11.cloned.1.call-done = bf16[768,4608]{0,1:T(8,128)(2,1)} async-done(((bf16[768,144]{0,1:T(8,128)(2,1)}), bf16[768,4608]{0,1:T(8,128)(2,1)}) %all-gather.11.cloned.1.call-update) | async-done | bytes 7077904 | tf_op jit(solution)/shard_map/all_gather | solution.py:103
  119.3 28.7 %all-gather.13.cloned.1.call-done = bf16[1536,768]{1,0:T(8,128)(2,1)} async-done(((bf16[384,768]{1,0:T(8,128)(2,1)}), bf16[1536,768]{1,0:T(8,128)(2,1)}) %all-gather.13.cloned.1.call-update) | async-done | bytes 2359312 | tf_op jit(solution)/shard_map/all_gather | solution.py:138
  151.4 36.8 %while.27 = (s32[]{:T(128)}, bf16[3,512,3,64]{1,3,2,0:T(8,128)(2,1)S(1)}, f32[3,3,512]{2,1,0:T(4,128)}, s32[3]{0:T(128)S(1)}, s32[1536]{0:T(1024)S(1)}, /*index=...) while((s32[]{:T(128)}, ...), condition=%wide.region_7.8_spmd, body=%wide.region_4.7_spmd.sunk | while | flops 633174528 | bytes 33098408 | solution.py:167
  193.0 84.2 %reduce-scatter.14.cloned.1.call-done = f32[384,768]{1,0:T(8,128)} async-done(((f32[1536,768]{1,0:T(8,128)}), f32[384,768]{1,0:T(8,128)}) %reduce-scatter.14.cloned.1.call-update) | async-done | bytes 1179664 | tf_op jit(solution)/shard_map/reduce_scatter | solution.py:169
  294.7 11.8 scatter_custom_fusion.1
  306.6 11.8 scatter_custom_fusion
  319.5 41.2 %all-reduce = bf16[6144]{0:T(1024)(128)(2,1)S(1)} all-reduce(bf16[6144]{0:T(1024)(128)(2,1)S(1)} %dynamic-update-slice), channel_id=1, replica_groups=mesh['dp'=8,'mp'=4] {'dp','mp'}, use_global_device_ids=true, to_apply=%add | all-reduce | flops 6144 | bytes 24576
  361.0 16.8 %gather_fusion = bf16[3840,768]{1,0:T(8,128)(2,1)} fusion(bf16[1536,768]{1,0:T(8,128)(2,1)} %all-gather.15.cloned.1.call-done, s32[4096]{0:T(1024)S(1)} %pad_clamp_fusion), kind=kCustom, calls=%fused_computation | custom fusion | bytes 11811840 | tf_op jit(solution)/shard_map/gather | solution.py:189
  377.7 17.4 %all-gather.21.cloned.1.call-done = bf16[8,768,768]{2,1,0:T(8,128)(2,1)} async-done(((bf16[8,96,768]{2,1,0:T(8,128)(2,1)}), bf16[8,768,768]{2,1,0:T(8,128)(2,1)}) %all-gather.21.cloned.1.call-update) | async-done | bytes 9437200 | tf_op jit(solution)/shard_map/all_gather | solution.py:120
  395.2 12.2 fusion.41
  407.4 49.0 %all-gather.23.cloned.1.call-done = bf16[8,768,768]{1,2,0:T(8,128)(2,1)} async-done(((bf16[8,768,96]{1,2,0:T(8,128)(2,1)}), bf16[8,768,768]{1,2,0:T(8,128)(2,1)}) %all-gather.23.cloned.1.call-update) | async-done | bytes 9437200 | tf_op jit(solution)/shard_map/all_gather | solution.py:121
  456.3 13.3 fusion.117
  480.8 11.4 gather_fusion.1
  492.2 16.8 %all-gather.25.cloned.1.call-done = bf16[1536,768]{1,0:T(8,128)(2,1)} async-done(((bf16[384,768]{1,0:T(8,128)(2,1)}), bf16[1536,768]{1,0:T(8,128)(2,1)}) %all-gather.25.cloned.1.call-update) | async-done | bytes 2359312 | tf_op jit(solution)/shard_map/all_gather | solution.py:208
  515.4 18.9 %all-gather.17.cloned.1.call-done = bf16[768,768]{1,0:T(8,128)(2,1)} async-done(((bf16[96,768]{1,0:T(8,128)(2,1)}), bf16[768,768]{1,0:T(8,128)(2,1)}) %all-gather.17.cloned.1.call-update) | async-done | bytes 1179664 | tf_op jit(solution)/shard_map/all_gather | solution.py:118
  544.6 11.8 scatter_custom_fusion.2
  556.5 12.6 gather_fusion.3
  569.2 17.6 %fusion.38 = bf16[8,480,768]{2,1,0:T(8,128)(2,1)} fusion(f32[8,480,768]{2,1,0:T(8,128)} %fusion.41, bf16[8,768,768]{1,2,0:T(8,128)(2,1)} %all-gather.23.cloned.1.call-done, bf16[8,480,768]{2,1,0:T(8,128)(2,1)} %bitcast.166, f32[8,480]{1,0:T(8,128)S(1)} %mul.644), kind=kOutput, calls=%fused_computation.57 | convolution fusion | flops 4597678080 | bytes 33045504 | tf_op jit(solution)/shard_map/ecd,efd->ecf/dot_general | solution.py:233
  589.0 14.6 fusion.142
  603.6 11.5 gather_fusion.4
  650.2 40.2 %reduce-scatter.18.cloned.1.call-done = bf16[384,768]{1,0:T(8,128)(2,1)} async-done(((bf16[1536,768]{1,0:T(8,128)(2,1)}), bf16[384,768]{1,0:T(8,128)(2,1)}) %reduce-scatter.18.cloned.1.call-update) | async-done | bytes 589840 | tf_op jit(solution)/shard_map/reduce_scatter | solution.py:259
  692.2 48.6 %reduce-scatter.16.cloned.1.call-done = bf16[384,768]{1,0:T(8,128)(2,1)} async-done(((bf16[1536,768]{1,0:T(8,128)(2,1)}), bf16[384,768]{1,0:T(8,128)(2,1)}) %reduce-scatter.16.cloned.1.call-update) | async-done | bytes 589840 | tf_op jit(solution)/shard_map/reduce_scatter | solution.py:201
  747.1 50.0 %all-gather.27.cloned.1.call-done = bf16[1536,768]{1,0:T(8,128)(2,1)} async-done(((bf16[384,768]{1,0:T(8,128)(2,1)}), bf16[1536,768]{1,0:T(8,128)(2,1)}) %all-gather.27.cloned.1.call-update) | async-done | bytes 2359312 | tf_op jit(solution)/shard_map/all_gather | solution.py:267
  800.6 102.8 %while.28 = (s32[]{:T(128)}, f32[1536,3,64]{0,2,1:T(8,128)S(1)}, f32[1536,3,64]{0,2,1:T(8,128)S(1)}, bf16[3,512,3,64]{1,3,2,0:T(8,128)(2,1)}, s32[3]{0:T(128)S(1...) while((s32[]{:T(128)}, f32[1536,3,64]{0,2,1:T(8,128)S(1)}, ...), condition=%wide.region_30.31_spmd.clone, body=%wide.region_28.30_spmd.clone.sunk | while | flops 1533540864 | bytes 155560816 | solution.py:305
  927.8 13.5 fusion.42
  941.9 16.2 %fusion.40 = f32[8,768,768]{2,1,0:T(8,128)} fusion(bf16[8,480,768]{2,1,0:T(8,128)(2,1)} %fusion.38, bf16[8,480,768]{2,1,0:T(8,128)(2,1)} %bitcast.164, pred[8,480]{1,0:T(8,128)(4,1)S(1)} %copy-done.54), kind=kOutput, calls=%fused_computation.66 | convolution fusion | flops 4532797440 | bytes 30674688 | tf_op jit(solution)/shard_map/ecd,ecf->edf/dot_general | solution.py:237
  982.3 40.2 %all-reduce.1 = f32[6144]{0:T(1024)S(1)} all-reduce(f32[6144]{0:T(1024)S(1)} %reshape.396), channel_id=7, replica_groups=mesh['dp'=8,'mp'=4] {'dp','mp'}, use_global_device_ids=true, to_apply=%region_35.36.clone | all-reduce | flops 6144 | bytes 49152
  1025.4 19.8 %reduce-scatter.34.cloned.1.call-done = f32[96,192]{1,0:T(8,128)} async-done(((f32[768,192]{1,0:T(8,128)}), f32[96,192]{1,0:T(8,128)}) %reduce-scatter.34.cloned.1.call-update) | async-done | bytes 73744
  1047.8 41.5 %reduce-scatter.24.cloned.1.call-done = f32[96,576]{1,0:T(8,128)} async-done(((f32[768,576]{1,0:T(8,128)}), f32[96,576]{1,0:T(8,128)}) %reduce-scatter.24.cloned.1.call-update) | async-done | bytes 221200 | tf_op jit(solution)/shard_map/reduce_scatter | solution.py:341
  1091.5 127.9 %reduce-scatter.32.cloned.1.call-done = f32[8,768,96]{1,2,0:T(8,128)} async-done(((f32[8,768,768]{1,2,0:T(8,128)}), f32[8,768,96]{1,2,0:T(8,128)}) %reduce-scatter.32.cloned.1.call-update) | async-done | bytes 2359312 | tf_op jit(solution)/shard_map/reduce_scatter | solution.py:346
  1227.0 122.6 %reduce-scatter.30.cloned.1.call-done = f32[8,96,768]{2,1,0:T(8,128)} async-done(((f32[8,768,768]{2,1,0:T(8,128)}), f32[8,96,768]{2,1,0:T(8,128)}) %reduce-scatter.30.cloned.1.call-update) | async-done | bytes 2359312 | tf_op jit(solution)/shard_map/reduce_scatter | solution.py:345
  1357.9 161.4 %reduce-scatter.22.cloned.1.call-done = f32[768,144]{0,1:T(8,128)} async-done(((f32[768,4608]{0,1:T(8,128)}), f32[768,144]{0,1:T(8,128)}) %reduce-scatter.22.cloned.1.call-update) | async-done | bytes 442384 | tf_op jit(solution)/shard_map/reduce_scatter | solution.py:352
  (402 shorter events, 354.1 us)
Async XLA Ops:
  7.2 79.6 %all-gather.11.cloned.1.call-start = ((), (), s32[]{:S(2)}) async-start(), calls=%async_computation.11 | async-start | bytes 7299072 | tf_op jit(solution)/shard_map/all_gather | solution.py:103
  9.0 139.0 %all-gather.13.cloned.1.call-start = ((), (), s32[]{:S(2)}) async-start(), calls=%async_computation.12 | async-start | bytes 2949120 | tf_op jit(solution)/shard_map/all_gather | solution.py:138
  20.7 71.1 %copy-start.61 = (bf16[24,768]{1,0:T(8,128)(2,1)}, bf16[24,768]{1,0:T(8,128)(2,1)S(1)}, u32[]{:S(2)}) copy-start(bf16[24,768]{1,0:T(8,128)(2,1)S(1)} %reshape.475) | copy-start | bytes 110596
  22.1 72.6 %copy-start.62 = (f32[384]{0:T(512)}, f32[384]{0:T(512)S(1)}, u32[]{:S(2)}) copy-start(f32[384]{0:T(512)S(1)} %broadcast_multiply_fusion.2) | copy-start | bytes 4612
  23.5 71.2 %copy-start.69 = (f32[384]{0:T(512)}, f32[384]{0:T(512)S(1)}, u32[]{:S(2)}) copy-start(f32[384]{0:T(512)S(1)} %fusion.106) | copy-start | bytes 4612
  98.8 178.3 %reduce-scatter.14.cloned.1.call-start = ((), (), s32[]{:S(2)}) async-start(), calls=%async_computation.13 | async-start | bytes 5898240 | tf_op jit(solution)/shard_map/reduce_scatter | solution.py:169
  108.6 80.4 %copy-start.28 = (bf16[192,768]{0,1:T(8,128)(2,1)}, bf16[192,768]{0,1:T(8,128)(2,1)S(1)}, u32[]{:S(2)}) copy-start(bf16[192,768]{0,1:T(8,128)(2,1)S(1)} %all_gather.43) | copy-start | bytes 884740
  192.9 87.1 %copy-start.24 = (bf16[384,768]{1,0:T(8,128)(2,1)S(1)}, bf16[384,768]{1,0:T(8,128)(2,1)}, u32[]{:S(2)}) copy-start(bf16[384,768]{1,0:T(8,128)(2,1)} %param.34) | copy-start | bytes 1769476
  192.9 168.0 %all-gather.15.cloned.1.call-start = ((), (), s32[]{:S(2)}) async-start(), calls=%async_computation.14 | async-start | bytes 2949120 | tf_op jit(solution)/shard_map/all_gather | solution.py:177
  283.3 111.8 %all-gather.21.cloned.1.call-start = ((), (), s32[]{:S(2)}) async-start(), calls=%async_computation.17 | async-start | bytes 10616832 | tf_op jit(solution)/shard_map/all_gather | solution.py:120
  286.4 170.0 %all-gather.23.cloned.1.call-start = ((), (), s32[]{:S(2)}) async-start(), calls=%async_computation.18 | async-start | bytes 10616832 | tf_op jit(solution)/shard_map/all_gather | solution.py:121
  287.6 221.4 %all-gather.25.cloned.1.call-start = ((), (), s32[]{:S(2)}) async-start(), calls=%async_computation.20 | async-start | bytes 2949120 | tf_op jit(solution)/shard_map/all_gather | solution.py:208
  288.4 246.0 %all-gather.17.cloned.1.call-start = ((), (), s32[]{:S(2)}) async-start(), calls=%async_computation.15 | async-start | bytes 1327104 | tf_op jit(solution)/shard_map/all_gather | solution.py:118
  289.1 297.6 %reduce-scatter.28.cloned.1.call-start = ((), (), s32[]{:S(2)}) async-start(), calls=%async_computation.27 | async-start | bytes 2654208 | tf_op jit(solution)/shard_map/reduce_scatter | solution.py:344
  318.5 76.7 %copy-start.53 = (pred[8,480]{1,0:T(8,128)(4,1)}, pred[8,480]{1,0:T(8,128)(4,1)S(1)}, u32[]{:S(2)}) copy-start(pred[8,480]{1,0:T(8,128)(4,1)S(1)} %broadcast_in_dim.79) | copy-start | bytes 11524
  543.8 82.5 %all-gather.19.cloned.1.call-start = ((), (), s32[]{:S(2)}) async-start(), calls=%async_computation.16 | async-start | bytes 1327104 | tf_op jit(solution)/shard_map/all_gather | solution.py:119
  589.0 101.5 %reduce-scatter.18.cloned.1.call-start = ((), (), s32[]{:S(2)}) async-start(), calls=%async_computation.21 | async-start | bytes 2949120 | tf_op jit(solution)/shard_map/reduce_scatter | solution.py:259
  642.2 98.6 %reduce-scatter.16.cloned.1.call-start = ((), (), s32[]{:S(2)}) async-start(), calls=%async_computation.19 | async-start | bytes 2949120 | tf_op jit(solution)/shard_map/reduce_scatter | solution.py:201
  650.1 90.7 %copy-start.65 = (f32[384]{0:T(512)S(1)}, f32[384]{0:T(512)}, u32[]{:S(2)}) copy-start(f32[384]{0:T(512)} %copy-done.64) | copy-start | bytes 4612
  650.2 147.0 %all-gather.27.cloned.1.call-start = ((), (), s32[]{:S(2)}) async-start(), calls=%async_computation.22 | async-start | bytes 2949120 | tf_op jit(solution)/shard_map/all_gather | solution.py:267
  747.0 212.9 %reduce-scatter.20.cloned.1.call-start = ((), (), s32[]{:S(2)}) async-start(), calls=%async_computation.23 | async-start | bytes 2949120 | tf_op jit(solution)/shard_map/reduce_scatter | solution.py:317
  912.9 110.2 %reduce-scatter.26.cloned.1.call-start = ((), (), s32[]{:S(2)}) async-start(), calls=%async_computation.26 | async-start | bytes 2654208 | tf_op jit(solution)/shard_map/reduce_scatter | solution.py:343
  918.5 126.7 %reduce-scatter.34.cloned.1.call-start = ((), (), s32[]{:S(2)}) async-start(), calls=%async_computation.30 | async-start | bytes 884736
  922.2 167.1 %reduce-scatter.24.cloned.1.call-start = ((), (), s32[]{:S(2)}) async-start(), calls=%async_computation.25 | async-start | bytes 2211840 | tf_op jit(solution)/shard_map/reduce_scatter | solution.py:341
  927.7 291.6 %reduce-scatter.32.cloned.1.call-start = ((), (), s32[]{:S(2)}) async-start(), calls=%async_computation.29 | async-start | bytes 21233664 | tf_op jit(solution)/shard_map/reduce_scatter | solution.py:346
  941.3 408.3 %reduce-scatter.30.cloned.1.call-start = ((), (), s32[]{:S(2)}) async-start(), calls=%async_computation.28 | async-start | bytes 21233664 | tf_op jit(solution)/shard_map/reduce_scatter | solution.py:345
  958.2 561.1 %reduce-scatter.22.cloned.1.call-start = ((), (), s32[]{:S(2)}) async-start(), calls=%async_computation.24 | async-start | bytes 14598144 | tf_op jit(solution)/shard_map/reduce_scatter | solution.py:352
  978.8 110.6 %copy-start.41 = (f32[96,576]{1,0:T(8,128)S(1)}, f32[96,576]{1,0:T(8,128)}, u32[]{:S(2)}) copy-start(f32[96,576]{1,0:T(8,128)} %param.44) | copy-start | bytes 663556
  982.0 237.3 %copy-start.22 = (f32[8,768,96]{1,2,0:T(8,128)S(1)}, f32[8,768,96]{1,2,0:T(8,128)}, u32[]{:S(2)}) copy-start(f32[8,768,96]{1,2,0:T(8,128)} %param.59) | copy-start | bytes 7077892
  1227.0 292.3 %copy-start.35 = (f32[768,144]{0,1:T(8,128)S(1)}, f32[768,144]{0,1:T(8,128)}, u32[]{:S(2)}) copy-start(f32[768,144]{0,1:T(8,128)} %param.38) | copy-start | bytes 1327108
  1227.0 292.3 %copy-start.46 = (f32[768,144]{0,1:T(8,128)S(1)}, f32[768,144]{0,1:T(8,128)}, u32[]{:S(2)}) copy-start(f32[768,144]{0,1:T(8,128)} %param.39) | copy-start | bytes 1327108
  1227.0 292.3 %copy-start.47 = (f32[768,144]{0,1:T(8,128)S(1)}, f32[768,144]{0,1:T(8,128)}, u32[]{:S(2)}) copy-start(f32[768,144]{0,1:T(8,128)} %param.40) | copy-start | bytes 1327108
  (81 other events, 1228.3 us)
Sparse Core Ops, SparseCore 0:
  11.4 75.3 all-gather.10
  98.9 49.0 all-gather.12
  193.0 84.0 reduce-scatter.13
  283.5 51.0 all-gather.14
  336.8 58.2 all-gather.20
  397.5 58.8 all-gather.22
  458.5 50.4 all-gather.24
  511.5 22.8 all-gather.16
  543.9 42.4 reduce-scatter.27
  589.1 24.0 all-gather.18
  642.3 48.0 reduce-scatter.17
  693.3 47.5 reduce-scatter.15
  747.1 49.9 all-gather.26
  913.0 46.8 reduce-scatter.19
  964.0 42.5 reduce-scatter.25
  1010.2 34.9 reduce-scatter.33
  1049.0 40.2 reduce-scatter.23
  1093.2 126.0 reduce-scatter.31
  1223.4 126.0 reduce-scatter.29
  1356.5 162.7 reduce-scatter.21
where the time goes:
time: 1540 us; the launch traced here: 1530 us
  waiting for transfers between devices  893 us (58%)
  matrix products  245 us (16%)
  local copies, waits for them, and re-layouts  140 us (9%)
  blocking collectives  112 us (7%)
  other arithmetic  109 us (7%)
  between operations  15.9 us (1%)
    reduce_scatter x1, waiting for transfers between devices, body(): lax.psum_scatter(grad_ada, ('dp', 'mp'), scatter_dimension=1, tiled=True)  161 us
    reduce_scatter x1, waiting for transfers between devices, body(): lax.psum_scatter(grad_expert_out, 'dp', scatter_dimension=2, tiled=True)  128 us
    reduce_scatter x1, waiting for transfers between devices, body(): lax.psum_scatter(grad_expert_in, 'dp', scatter_dimension=1, tiled=True)  123 us
    reduce_scatter x1, waiting for transfers between devices, body(): lax.psum_scatter(jnp.dot(mixed_rows, proj_here, preferred_element_type=jn...  84.2 us
    unnamed x2, blocking collectives  81.4 us
    all_gather x1, waiting for transfers between devices, body(): lax.all_gather(ada_weight.astype(jnp.bfloat16), ('dp', 'mp'), axis=1, til...  63.3 us
    all_gather x1, waiting for transfers between devices, body(): grad_attn_all = lax.all_gather(grad_attn, 'mp', axis=0, tiled=True)  50 us
    all_gather x1, waiting for transfers between devices, body(): lax.all_gather(expert_out_weight.astype(jnp.bfloat16), 'dp', axis=2, tile...  49 us
  transfers between devices with their start and end apart: 20, of which 16 were waited for; matrix products, arithmetic and copies ran while one was open for 19% of the time, Pallas kernels for 0%

commit v1 on v0

v1 whole, which is shorter than its diff:
```python
import jax
import jax.numpy as jnp
from jax import lax
from jax.sharding import PartitionSpec as P

H = 12
HD = 64
E = 8
STEP = 10

beta_one = 0.9
beta_two = 0.95
epsilon = 1e-08
weight_decay = 0.1
norm_floor = 1e-06
highest = lax.Precision.HIGHEST
f32 = jnp.float32
bf16 = jnp.bfloat16


def norm_parts(values):
    centred = values - jnp.mean(values, axis=1, keepdims=True)
    inverse = lax.rsqrt(jnp.mean(centred * centred, axis=1, keepdims=True) + norm_floor)
    return centred * inverse, inverse


def norm_back(normed, inverse, gradient):
    first = jnp.mean(gradient, axis=1, keepdims=True)
    second = jnp.mean(gradient * normed, axis=1, keepdims=True)
    return inverse * (gradient - first - normed * second)


def gelu_back(before, gradient):
    return jax.vjp(jax.nn.gelu, before)[1](gradient)[0]


def by_item(table, segment):
    picked = table[0][None, :]
    for item in range(1, table.shape[0]):
        picked = jnp.where(segment[:, None] >= item, table[item][None, :], picked)
    return picked


def line_gather(block):
    width = lax.axis_size("mp")
    rank = lax.axis_index("mp")
    ups, downs = [block], [block]
    for step in range(1, width):
        up_pairs = [(i, i + 1) for i in range(step - 1, width - 1)]
        down_pairs = [(i + 1, i) for i in range(width - step)]
        ups.append(lax.ppermute(ups[-1], "mp", up_pairs))
        downs.append(lax.ppermute(downs[-1], "mp", down_pairs))
    rows = block.shape[0]
    whole = jnp.zeros((rows * width,) + block.shape[1:], block.dtype)
    for offset in range(width):
        piece = block if offset == 0 else jnp.where(rank >= offset, ups[offset], downs[width - offset])
        owner = lax.rem(rank - offset + width, width)
        whole = lax.dynamic_update_slice_in_dim(whole, piece, owner * rows, 0)
    return whole


def line_scatter(partial, axis=0):
    width = lax.axis_size("mp")
    rank = lax.axis_index("mp")
    extent = partial.shape[axis] // width

    def part(index):
        index = jnp.clip(index, 0, width - 1)
        return lax.dynamic_slice_in_dim(partial, index * extent, extent, axis)

    up, down = None, None
    for step in range(1, width):
        up_send, down_send = part(rank + width - step), part(rank - width + step)
        if up is not None:
            up_send = (up_send.astype(f32) + up.astype(f32)).astype(bf16)
            down_send = (down_send.astype(f32) + down.astype(f32)).astype(bf16)
        up = lax.ppermute(up_send, "mp", [(i, i + 1) for i in range(step)])
        down = lax.ppermute(down_send, "mp", [(i, i - 1) for i in range(width - step, width)])
    return part(rank).astype(f32) + up.astype(f32) + down.astype(f32)


def adamw_update(master, first, second, gradient, fan_in):
    step_rate = 0.5 * fan_in ** (-0.5)
    first_new = beta_one * first + (1.0 - beta_one) * gradient
    second_new = beta_two * second + (1.0 - beta_two) * gradient * gradient
    first_hat = first_new / (1.0 - beta_one**STEP)
    second_hat = second_new / (1.0 - beta_two**STEP)
    master_new = master - step_rate * (
        first_hat / (jnp.sqrt(second_hat) + epsilon) + weight_decay * master
    )
    return (master_new, first_new, second_new, master_new.astype(bf16))


def body(
    patches,
    cotangent,
    conditioning,
    lengths,
    routes,
    ada_weight,
    ada_first,
    ada_second,
    router_weight,
    router_first,
    router_second,
    qkv_weight,
    qkv_first,
    qkv_second,
    proj_weight,
    proj_first,
    proj_second,
    shared_in_weight,
    shared_in_first,
    shared_in_second,
    shared_out_weight,
    shared_out_first,
    shared_out_second,
    expert_in_weight,
    expert_in_first,
    expert_in_second,
    expert_out_weight,
    expert_out_first,
    expert_out_second,
):
    rows, D = patches.shape
    width = lax.axis_size("mp")
    n_dp = lax.axis_size("dp")
    devices = width * n_dp
    group = rows * width
    capacity = 5 * group // 16
    heads_here = H // width
    qrows = 512
    block_count = group // qrows
    scaling = HD ** (-0.5)
    model_rank = lax.axis_index("mp")
    item_count = lengths.shape[1]
    hidden = shared_in_weight.shape[1]
    ada_cols = ada_weight.shape[1]
    router_cols = router_weight.shape[0]

    def mine(values, axis=0):
        extent = values.shape[axis] // width
        return lax.dynamic_slice_in_dim(values, model_rank * extent, extent, axis)

    patches_all = line_gather(patches)
    cond_all = lax.all_gather(conditioning, "dp", axis=0, tiled=True)
    qkv_here = lax.all_gather(qkv_weight.astype(bf16), "dp", axis=0, tiled=True)
    proj_rows = line_gather(proj_weight.astype(bf16))
    proj_t = lax.all_gather(proj_rows.T, "dp", axis=0, tiled=True)
    cot_all = line_gather(cotangent)
    out_slab = jnp.concatenate(
        [
            jnp.swapaxes(expert_out_weight.astype(bf16), 1, 2),
            shared_out_weight.astype(bf16).T[None],
        ],
        axis=0,
    )
    in_slab = jnp.concatenate(
        [expert_in_weight.astype(bf16), shared_in_weight.astype(bf16)[None]], axis=0
    )
    out_t = lax.all_gather(out_slab, "dp", axis=1, tiled=True)
    in_w = lax.all_gather(in_slab, "dp", axis=1, tiled=True)

    cond_act = jax.nn.silu(cond_all.astype(f32)).astype(bf16)
    columns = jnp.dot(cond_act, ada_weight.astype(bf16), preferred_element_type=f32)
    columns = jnp.repeat(columns.reshape(n_dp, item_count * ada_cols), width, axis=0)
    router_low = router_weight.astype(bf16).astype(f32)
    payload = jnp.concatenate(
        [columns, jnp.broadcast_to(router_low[None], (devices, router_cols))], axis=1
    )
    received = lax.all_to_all(payload, ("dp", "mp"), 0, 0, tiled=True)
    modulation = (
        received[:, : item_count * ada_cols]
        .reshape(devices, item_count, ada_cols)
        .transpose(1, 0, 2)
        .reshape(item_count, devices * ada_cols)
    )
    router_matrix = received[:, item_count * ada_cols :].reshape(D, E).astype(bf16)

    bounds = jnp.cumsum(lengths[0])
    places = jnp.arange(group, dtype=jnp.int32)
    segment = jnp.sum((places[:, None] >= bounds[None, :]).astype(jnp.int32), axis=1)
    segment_mine = mine(segment)
    terms = jnp.split(modulation, 6, axis=1)
    shift_one, scale_one, gate_one, shift_two, scale_two, gate_two = [
        by_item(t, segment) for t in terms
    ]
    _, scale_one_mine, gate_one_mine, _, scale_two_mine, gate_two_mine = [
        by_item(t, segment_mine) for t in terms
    ]

    names = (routes[:, :, None] == jnp.arange(E, dtype=jnp.int32)[None, None, :]).any(axis=1)
    below = (places[:, None] > places[None, :]).astype(bf16)
    earlier = jnp.dot(below, names.astype(bf16), preferred_element_type=f32).astype(jnp.int32)
    place_of = jnp.where(names, earlier, -1).T
    picks = place_of[:, None, :] == jnp.arange(capacity, dtype=jnp.int32)[None, :, None]
    picks_low = picks.astype(bf16)

    normed_one, _ = norm_parts(patches_all.astype(f32))
    h_one_all = (normed_one * (1.0 + scale_one) + shift_one).astype(bf16)
    qkv = jnp.dot(h_one_all, qkv_here, preferred_element_type=f32).astype(bf16)
    qkv = qkv.reshape(group, heads_here, 3, HD)
    queries, key_rows, value_rows = qkv[:, :, 0], qkv[:, :, 1], qkv[:, :, 2]
    starts = jnp.arange(block_count, dtype=jnp.int32) * qrows

    def block_scores(row_start):
        query_rows = lax.dynamic_slice_in_dim(queries, row_start, qrows, 0)
        query_items = lax.dynamic_slice_in_dim(segment, row_start, qrows, 0)
        scores = (
            jnp.einsum("qhd,khd->hqk", query_rows, key_rows, preferred_element_type=f32) * scaling
        )
        allowed = query_items[:, None] == segment[None, :]
        return (query_rows, jnp.where(allowed[None], scores, -1e30))

    def attend_block(row_start):
        query_rows, scores = block_scores(row_start)
        row_peak = jnp.max(scores, axis=2, keepdims=True)
        exps = jnp.exp(scores - row_peak)
        row_total = jnp.sum(exps, axis=2, keepdims=True)
        attn_probs = (exps / row_total).astype(bf16)
        mixed_block = jnp.einsum("hqk,khd->qhd", attn_probs, value_rows, preferred_element_type=f32)
        return (mixed_block.astype(bf16), (row_peak + jnp.log(row_total))[:, :, 0])

    mixed_blocks, log_totals = lax.map(attend_block, starts)
    mixed_here = mixed_blocks.reshape(group, heads_here * HD)
    mixed_parts = line_gather(mixed_here)
    mixed_all = (
        mixed_parts.reshape(width, group, heads_here * HD).transpose(1, 0, 2).reshape(group, H * HD)
    )
    attn_branch = jnp.einsum("gc,dc->gd", mixed_all, proj_t, preferred_element_type=f32)
    x_one = patches_all.astype(f32) + gate_one * attn_branch
    normed_two, _ = norm_parts(x_one)
    h_two = (normed_two * (1.0 + scale_two) + shift_two).astype(bf16)

    grad_branch = (gate_two * cot_all.astype(f32)).astype(bf16)
    branch_slots = jnp.einsum("ect,td->ecd", picks_low, grad_branch, preferred_element_type=f32)
    branch_slots = branch_slots.astype(bf16)
    back_slots = jnp.einsum("ecd,edf->ecf", branch_slots, out_t[:E], preferred_element_type=f32)
    back_shared = jnp.dot(grad_branch, out_t[E], preferred_element_type=f32)

    logits = jnp.dot(h_two, router_matrix, preferred_element_type=f32).T
    names_t = place_of >= 0
    peak = jnp.max(jnp.where(names_t, logits, -jnp.inf), axis=0, keepdims=True)
    weights = jnp.where(names_t, jnp.exp(logits - peak), 0.0)
    gates = weights / jnp.sum(weights, axis=0, keepdims=True)
    gate_slots = jnp.sum(jnp.where(picks, gates[:, None, :], 0.0), axis=2)
    shared_pre = jnp.dot(h_two, in_w[E], preferred_element_type=f32)
    shared_act = jax.nn.gelu(shared_pre).astype(bf16)
    grad_shared_pre = gelu_back(shared_pre, back_shared).astype(bf16)
    dispatched = jnp.einsum(
        "ect,td->ecd", picks_low, h_two, preferred_element_type=f32
    ).astype(bf16)
    expert_pre = jnp.einsum("ecd,edf->ecf", dispatched, in_w[:E], preferred_element_type=f32)
    expert_act = jax.nn.gelu(expert_pre).astype(bf16)
    grad_expert_pre = gelu_back(expert_pre, gate_slots[:, :, None] * back_slots).astype(bf16)
    grad_gate_slots = jnp.sum(back_slots * expert_act.astype(f32), axis=2)
    grad_gates = jnp.sum(jnp.where(picks, grad_gate_slots[:, :, None], 0.0), axis=1)
    grad_logits = gates * (grad_gates - jnp.sum(gates * grad_gates, axis=0, keepdims=True))
    grad_dispatched = jnp.einsum(
        "ecf,edf->ecd", grad_expert_pre, in_w[:E], preferred_element_type=f32
    ).astype(bf16)
    grad_h_two = (
        jnp.einsum("gf,df->gd", grad_shared_pre, in_w[E], preferred_element_type=f32)
        + jnp.einsum("ect,ecd->td", picks_low, grad_dispatched, preferred_element_type=f32)
        + jnp.einsum("eg,de->gd", grad_logits, router_matrix.astype(f32), precision=highest)
    )
    grad_h_two_mine = line_scatter(grad_h_two.astype(bf16))

    grad_res = (gate_slots[:, :, None] * branch_slots.astype(f32)).astype(bf16)
    grad_out_slab = jnp.concatenate(
        [
            jnp.einsum("ecd,ecf->edf", grad_res, expert_act, preferred_element_type=f32).astype(bf16),
            jnp.einsum("gd,gf->df", grad_branch, shared_act, preferred_element_type=f32).astype(bf16)[
                None
            ],
        ],
        axis=0,
    )
    grad_in_slab = jnp.concatenate(
        [
            jnp.einsum("ecd,ecf->edf", dispatched, grad_expert_pre, preferred_element_type=f32).astype(
                bf16
            ),
            jnp.einsum("gd,gf->df", h_two, grad_shared_pre, preferred_element_type=f32).astype(bf16)[
                None
            ],
        ],
        axis=0,
    )
    grad_out_mine = lax.psum_scatter(grad_out_slab, "dp", scatter_dimension=1, tiled=True).astype(f32)
    grad_in_mine = lax.psum_scatter(grad_in_slab, "dp", scatter_dimension=1, tiled=True).astype(f32)
    grad_router = jnp.einsum("gd,eg->de", h_two.astype(f32), grad_logits, precision=highest)
    expert_res = jnp.einsum("ecf,edf->ecd", expert_act, out_t[:E], preferred_element_type=f32)
    expert_res = (gate_slots[:, :, None] * expert_res).astype(bf16)
    mlp_part = jnp.einsum("gf,df->gd", shared_act, out_t[E], preferred_element_type=f32) + jnp.einsum(
        "ect,ecd->td", picks_low, expert_res, preferred_element_type=f32
    )
    mlp_branch = line_scatter(mlp_part.astype(bf16))

    x_one_mine = mine(x_one)
    attn_mine = mine(attn_branch)
    grad_out = cotangent.astype(f32)
    outcome = x_one_mine + gate_two_mine * mlp_branch
    grad_gate_two = grad_out * mlp_branch
    normed_two_mine, inverse_two = norm_parts(x_one_mine)
    grad_scale_two = grad_h_two_mine * normed_two_mine
    grad_x_one = grad_out + norm_back(
        normed_two_mine, inverse_two, grad_h_two_mine * (1.0 + scale_two_mine)
    )
    grad_gate_one = grad_x_one * attn_mine
    grad_attn = (gate_one_mine * grad_x_one).astype(bf16)
    grad_mixed_mine = jnp.dot(grad_attn, proj_t, preferred_element_type=f32).astype(bf16)
    grad_mixed = lax.all_to_all(
        grad_mixed_mine.reshape(rows, width, heads_here * HD).transpose(1, 0, 2),
        "mp",
        0,
        0,
        tiled=True,
    ).reshape(group, heads_here, HD)
    grad_proj_t = jnp.einsum("gd,gc->dc", grad_attn, mine(mixed_all), preferred_element_type=f32)
    grad_proj_t = line_scatter(grad_proj_t.astype(bf16), axis=1)

    def attend_back(carry, inputs):
        grad_keys, grad_values = carry
        row_start, log_block = inputs
        query_rows, scores = block_scores(row_start)
        grad_rows = lax.dynamic_slice_in_dim(grad_mixed, row_start, qrows, 0)
        soft_rows = jnp.exp(scores - log_block[:, :, None])
        soft_low = soft_rows.astype(bf16)
        grad_values = grad_values + jnp.einsum(
            "hqk,qhd->khd", soft_low, grad_rows, preferred_element_type=f32
        )
        grad_soft = jnp.einsum("qhd,khd->hqk", grad_rows, value_rows, preferred_element_type=f32)
        middle = jnp.sum(soft_rows * grad_soft, axis=2, keepdims=True)
        grad_scores = (soft_rows * (grad_soft - middle)).astype(bf16)
        grad_query = (
            jnp.einsum("hqk,khd->qhd", grad_scores, key_rows, preferred_element_type=f32) * scaling
        )
        grad_keys = (
            grad_keys
            + jnp.einsum("hqk,qhd->khd", grad_scores, query_rows, preferred_element_type=f32)
            * scaling
        )
        return ((grad_keys, grad_values), grad_query)

    zero_rows = jnp.zeros((group, heads_here, HD), f32)
    (grad_keys, grad_values), grad_queries = lax.scan(
        attend_back, (zero_rows, zero_rows), (starts, log_totals)
    )
    grad_queries = grad_queries.reshape(group, heads_here, HD)
    grad_qkv = (
        jnp.stack([grad_queries, grad_keys, grad_values], axis=2)
        .astype(bf16)
        .reshape(group, heads_here * 3 * HD)
    )
    grad_h_one = line_scatter(
        jnp.einsum("gc,dc->gd", grad_qkv, qkv_here, preferred_element_type=f32).astype(bf16)
    )
    grad_qkv_weight = jnp.einsum("gd,gc->dc", h_one_all, grad_qkv, preferred_element_type=f32)
    grad_attn_slab = jnp.concatenate([grad_qkv_weight.astype(bf16), grad_proj_t.astype(bf16)], axis=1)
    grad_attn_mine = lax.psum_scatter(grad_attn_slab, "dp", scatter_dimension=0, tiled=True).astype(f32)

    normed_one_mine, inverse_one = norm_parts(patches.astype(f32))
    grad_scale_one = grad_h_one * normed_one_mine
    grad_states = grad_x_one + norm_back(
        normed_one_mine, inverse_one, grad_h_one * (1.0 + scale_one_mine)
    )
    grad_token_mod = jnp.concatenate(
        [grad_h_one, grad_scale_one, grad_gate_one, grad_h_two_mine, grad_scale_two, grad_gate_two],
        axis=1,
    )
    marks_mine = (
        segment_mine[:, None] == jnp.arange(item_count, dtype=jnp.int32)[None, :]
    ).astype(f32)
    grad_modulation = jnp.einsum("ti,tc->ic", marks_mine, grad_token_mod, precision=highest)
    payload = jnp.concatenate(
        [
            grad_modulation.reshape(item_count, devices, ada_cols)
            .transpose(1, 0, 2)
            .reshape(devices, item_count * ada_cols),
            grad_router.reshape(devices, router_cols),
        ],
        axis=1,
    )
    received = lax.all_to_all(payload, ("dp", "mp"), 0, 0, tiled=True)
    router_grad = jnp.sum(received[:, item_count * ada_cols :], axis=0)
    columns = jnp.sum(
        received[:, : item_count * ada_cols].reshape(n_dp, width, item_count, ada_cols), axis=1
    ).reshape(n_dp * item_count, ada_cols)
    ada_grad = jnp.einsum("id,ic->dc", cond_act.astype(f32), columns, precision=highest)

    qkv_cols = qkv_weight.shape[1]
    gradients = (
        ada_grad,
        router_grad,
        grad_attn_mine[:, :qkv_cols],
        grad_attn_mine[:, qkv_cols:].T,
        grad_in_mine[E],
        grad_out_mine[E].T,
        grad_in_mine[:E],
        jnp.swapaxes(grad_out_mine[:E], 1, 2),
    )
    states_of = (
        (ada_weight, ada_first, ada_second),
        (router_weight, router_first, router_second),
        (qkv_weight, qkv_first, qkv_second),
        (proj_weight, proj_first, proj_second),
        (shared_in_weight, shared_in_first, shared_in_second),
        (shared_out_weight, shared_out_first, shared_out_second),
        (expert_in_weight, expert_in_first, expert_in_second),
        (expert_out_weight, expert_out_first, expert_out_second),
    )
    total_hidden = float(hidden * width)
    fan_ins = (D, D, D, 8.0 * D / group, D, total_hidden, D, total_hidden)
    updates = []
    for (master, first, second), gradient, fan_in in zip(states_of, gradients, fan_ins):
        updates.extend(adamw_update(master, first, second, gradient, float(fan_in)))
    return tuple([outcome.astype(bf16), grad_states.astype(bf16)] + updates)


def solution(mesh):
    tokens, data = P(("dp", "mp"), None), P("dp", None)
    ada, router = P(None, ("dp", "mp")), P(("dp", "mp"))
    deep, wide = P("dp", "mp"), P("mp", "dp")
    deep_experts, wide_experts = P(None, "dp", "mp"), P(None, "mp", "dp")
    kinds = (ada, router, deep, wide, deep, wide, deep_experts, wide_experts)
    in_specs = (tokens, tokens, data, data, data) + tuple(k for k in kinds for _ in range(3))
    out_specs = (tokens, tokens) + tuple(k for k in kinds for _ in range(4))
    return jax.shard_map(body, mesh=mesh, in_specs=in_specs, out_specs=out_specs, check_vma=False)
```

time: 1540 us -> 888 us (0.58)
  waiting for transfers between devices: 893 us -> 180 us
  starting transfers between devices: 1.58 us -> 137 us
  blocking collectives: 112 us -> 24 us
  local copies, waits for them, and re-layouts: 140 us -> 83 us
  other arithmetic: 109 us -> 157 us
  matrix products: 245 us -> 269 us
    reduce_scatter x10 -> x2, waiting for transfers between devices: 628 us -> 65.3 us  [the longest x1 65.3 us: body(): lax.psum_scatter(grad_in_slab, 'dp', scatter_dimension=1, tiled=True)]
    all_gather x9 -> x3, waiting for transfers between devices: 244 us -> 0.02 us  [the longest x1 0.02 us: body(): in_w = lax.all_gather(in_slab, 'dp', axis=1, tiled=True)]
    ppermute x0 -> x48, starting transfers between devices: none -> 118 us  [the longest x12 57.4 us: line_scatter(): up = lax.ppermute(up_send, 'mp', [(i, i + 1) for i in range(step)])]
    ppermute x0 -> x48, waiting for transfers between devices: none -> 109 us  [the longest x12 56.6 us: line_scatter(): up = lax.ppermute(up_send, 'mp', [(i, i + 1) for i in range(step)])]
    unnamed x2 -> x0, blocking collectives: 81.4 us -> none
    gather x6 -> x0, local copies, waits for them, and re-layouts: 74.6 us -> none  [the longest x1 16.8 us: body(): h_two_all[slot_token]]
    dot_general x32 -> x35, matrix products: 181 us -> 228 us  [the longest x6 31.8 us: block_scores(): jnp.einsum('qhd,khd->hqk', query_rows, key_rows, preferred_element_type=f32)]
    scatter x3 -> x0, local copies, waits for them, and re-layouts: 35.4 us -> none  [the longest x1 11.8 us: slot_tables(): jnp.zeros((E * capacity,), jnp.int32).at[destination].set(owner_rows)]
  transfers between devices with their start and end apart: 20 -> 57, of which waited for: 16 -> 22; matrix products, arithmetic and copies ran while one was open for 19% -> 45% of each run, Pallas kernels for 0% -> 0%
where the time goes in v1:
time: 888 us; the launch traced here: 879 us
  matrix products  269 us (30%)
  waiting for transfers between devices  180 us (20%)
  other arithmetic  157 us (18%)
  starting transfers between devices  137 us (15%)
  local copies, waits for them, and re-layouts  83 us (9%)
  blocking collectives  24 us (3%)
  between operations  16.8 us (2%)
  loops' own time  12 us (1%)
    reduce_scatter x1, waiting for transfers between devices, body(): lax.psum_scatter(grad_in_slab, 'dp', scatter_dimension=1, tiled=True)  65.3 us
    ppermute x12, starting transfers between devices, line_scatter(): up = lax.ppermute(up_send, 'mp', [(i, i + 1) for i in range(step)])  57.4 us
    ppermute x12, waiting for transfers between devices, line_scatter(): up = lax.ppermute(up_send, 'mp', [(i, i + 1) for i in range(step)])  56.6 us
    ppermute x12, waiting for transfers between devices, line_gather(): downs.append(lax.ppermute(downs[-1], 'mp', down_pairs))  40.2 us
    dot_general x6, matrix products, block_scores(): jnp.einsum('qhd,khd->hqk', query_rows, key_rows, preferred_element_type=f32)  31.8 us
    ppermute x12, starting transfers between devices, line_gather(): ups.append(lax.ppermute(ups[-1], 'mp', up_pairs))  29.2 us
    convert_element_type x3, other arithmetic, attend_back(): grad_scores = (soft_rows * (grad_soft - middle)).astype(bf16)  28.2 us
    unnamed x264, local copies, waits for them, and re-layouts  27.9 us
  transfers between devices with their start and end apart: 57, of which 22 were waited for; matrix products, arithmetic and copies ran while one was open for 45% of the time, Pallas kernels for 0%

profile of v1, /device:TPU:0, one launch (start us, length us, event | category | flops | bytes accessed | tf_op | source)
XLA Modules:
  0.0 878.6 jit_solution(9846174873658904522)
XLA Ops:
  52.0 10.1 %all-gather = bf16[8,3,768]{2,1,0:T(4,128)(2,1)} all-gather(bf16[1,3,768]{2,1,0:T(4,128)(2,1)S(1)} %bitcast.229), channel_id=1, replica_groups=mesh['dp'=8,'mp'=4] {'dp'}, dimensions={0}, use_global_device_ids=true | all-gather | bytes 41472 | tf_op jit(solution)/shard_map/all_gather | solution.py:146
  78.5 13.9 %all_gather.16 = bf16[768,576]{1,0:T(8,128)(2,1)} all-gather(bf16[96,576]{1,0:T(8,128)(2,1)S(1)} %convert_element_type.392), channel_id=1, replica_groups=mesh['dp'=8,'mp'=4] {'dp'}, dimensions={0}, use_global_device_ids=true | all-gather | bytes 995328 | tf_op jit(solution)/shard_map/all_gather | solution.py:147
  103.3 9.4 %collective-permute-done.3 = bf16[384,768]{0,1:T(8,128)(2,1)} collective-permute-done((bf16[384,768]{0,1:T(8,128)(2,1)}, bf16[384,768]{0,1:T(8,128)(2,1)}, u32[]{:S(2)}, u32[]{:S(2)}) %collective-permute-start.3) | collective-permute-done | bytes 589856 | tf_op jit(solution)/shard_map/ppermute | solution.py:52
  126.5 43.4 %while.27 = (s32[]{:T(128)}, bf16[3,512,3,64]{1,3,2,0:T(8,128)(2,1)}, f32[3,3,512]{2,1,0:T(4,128)}, s32[3]{0:T(128)}, s32[1536]{0:T(1024)S(1)}, /*index=5*/bf16[...) while((s32[]{:T(128)}, ...), condition=%wide.region_7.8_spmd, body=%wide.region_4.7_spmd.sunk | while | flops 633174528 | bytes 33093812 | solution.py:224
  192.7 11.4 %collective-permute-done.27 = bf16[384,768]{0,1:T(8,128)(2,1)} collective-permute-done((bf16[384,768]{0,1:T(8,128)(2,1)}, bf16[384,768]{0,1:T(8,128)(2,1)}, u32[]{:S(2)}, u32[]{:S(2)}) %collective-permute-start.27) | collective-permute-done | bytes 589856 | tf_op jit(solution)/shard_map/ppermute | solution.py:52
  216.5 15.1 %fusion.76 = bf16[8,480,768]{2,1,0:T(8,128)(2,1)} fusion(s32[8,1536]{1,0:T(8,128)S(1)} %copy-done.62, bf16[1536,768]{0,1:T(8,128)(2,1)} %select_dynamic-update-slice_fusion, f32[768]{0:T(1024)S(1)} %copy-done.95, f32[768]{0:T(1024)S(1)} %copy-done.97, f32[768]{0:T(1024)S(1)} %copy-done.93, pred[1536]{0:T(1024)(128)(4,1)S(1)} %copy-done.91, ...), kind=kOutput, calls=%fused_computation.112 | convolution fusion | flops 9074442240 | bytes 8318976 | tf_op jit(solution)/shard_map/ect,td->ecd/dot_general | solution.py:236
  263.3 12.3 %fusion.75 = bf16[8,480,768]{2,1,0:T(8,128)(2,1)} fusion(s32[8,1536]{1,0:T(8,128)S(1)} %copy-done.62, bf16[1536,768]{0,1:T(8,128)(2,1)S(1)} %add_convert_fusion), kind=kOutput, calls=%fused_computation.111 | convolution fusion | flops 9068544000 | bytes 8306688 | tf_op jit(solution)/shard_map/ect,td->ecd/dot_general | solution.py:250
  275.6 14.5 %fusion.54 = f32[8,480,768]{2,1,0:T(8,128)} fusion(bf16[8,480,768]{2,1,0:T(8,128)(2,1)} %fusion.75, bf16[9,768,768]{2,1,0:T(8,128)(2,1)} %all-gather.7.cloned.1.call-done), kind=kOutput, calls=%fused_computation.74 | convolution fusion | flops 4529848320 | bytes 27131904 | tf_op jit(solution)/shard_map/ecd,edf->ecf/dot_general | solution.py:253
  290.1 15.6 %multiply_reduce_fusion.1 = (f32[8,480]{1,0:T(8,128)S(1)}, f32[8,480,768]{2,1,0:T(8,128)}) fusion(f32[8,480,768]{2,1,0:T(8,128)} %fusion.54, bf16[8,480,768]{2,1,0:T(8,128)(2,1)} %fusion.76, bf16[9,768,768]{2,1,0:T(8,128)(2,1)} %all-gather.9.cloned.1.call-done), kind=kOutput, calls=%fused_computation.57 | convolution fusion | flops 4565233664 | bytes 38943744 | tf_op jit(solution)/shard_map/ecd,edf->ecf/dot_general | solution.py:238
  312.0 14.9 %fusion.42 = bf16[8,480,768]{2,1,0:T(8,128)(2,1)} fusion(f32[8,480,768]{2,1,0:T(8,128)} %fusion.54, f32[8,480,768]{2,1,0:T(8,128)} %get-tuple-element.480, f32[8,480]{1,0:T(8,128)S(1)} %get-tuple-element.370), kind=kLoop, calls=%fused_computation.55 | loop fusion | flops 61931520 | bytes 29506560 | tf_op jit(solution)/shard_map/convert_element_type | solution.py:255
  330.2 8.8 fusion.71
  345.8 23.5 %fusion.32 = f32[1536,768,1]{0,1,2:T(8,128)} fusion(s32[8,1536]{1,0:T(8,128)S(1)} %copy-done.62, bf16[8,480,768]{2,1,0:T(8,128)(2,1)} %fusion.42, bf16[9,768,768]{2,1,0:T(8,128)(2,1)} %all-gather.7.cloned.1.call-done), kind=kOutput, calls=%fused_computation.43 | convolution fusion | flops 13598392320 | bytes 20103168 | tf_op jit(solution)/shard_map/ect,ecd->td/dot_general | solution.py:264
  387.4 22.2 %fusion.74 = bf16[1536,768]{0,1:T(8,128)(2,1)} fusion(f32[1536,768]{0,1:T(8,128)} %fusion.107, f32[8,480]{1,0:T(8,128)S(1)} %get-tuple-element.370, s32[8,1536]{1,0:T(8,128)S(1)} %copy-done.62, bf16[9,768,768]{2,1,0:T(8,128)(2,1)} %all-gather.9.cloned.1.call-done, f32[8,480,768]{2,1,0:T(8,128)} %fusion.54), kind=kOutput, calls=%fused_computation.103 | convolution fusion | flops 13630242816 | bytes 28376064 | tf_op jit(solution)/shard_map/ect,ecd->td/dot_general | solution.py:295
  442.2 7.6 collective-permute-done.19
  471.3 9.1 %collective-permute-done.20 = bf16[384,768]{0,1:T(8,128)(2,1)S(1)} collective-permute-done((bf16[384,768]{0,1:T(8,128)(2,1)S(1)}, bf16[384,768]{0,1:T(8,128)(2,1)S(1)}, u32[]{:S(2)}, u32[]{:S(2)}) %collective-permute-start.20) | collective-permute-done | bytes 589856 | tf_op jit(solution)/shard_map/ppermute | solution.py:77
  480.6 8.2 collective-permute-done.23
  496.0 7.3 collective-permute-start.42
  525.4 6.7 collective-permute-start.44
  538.2 97.0 %while.28 = (s32[]{:T(128)}, f32[1536,3,64]{0,2,1:T(8,128)S(1)}, f32[1536,3,64]{0,2,1:T(8,128)S(1)}, bf16[3,512,3,64]{1,3,2,0:T(8,128)(2,1)}, s32[3]{0:T(128)S(1...) while((s32[]{:T(128)}, f32[1536,3,64]{0,2,1:T(8,128)S(1)}, ...), condition=%wide.region_25.26_spmd.clone, body=%wide.region_23.25_spmd.clone.sunk | while | flops 1533540864 | bytes 141404592 | solution.py:347
  544.5 7.5 multiply_reduce_fusion.7
  552.0 9.4 %multiply_convert_fusion.25 = bf16[3,512,1536]{2,1,0:T(8,128)(2,1)} fusion(f32[3,512,1536]{2,1,0:T(8,128)} %get-tuple-element.606, f32[3,512,1536]{2,1,0:T(8,128)} %copy-done, f32[3,512]{1,0:T(4,128)S(1)} %get-tuple-element.607), kind=kLoop, calls=%fused_computation.16.clone.1 | loop fusion | flops 7077888 | bytes 23599104 | tf_op jit(solution)/shard_map/while/body/eval_jaxpr/convert_element_type | solution.py:335
  576.9 7.5 multiply_reduce_fusion.7
  584.4 9.4 %multiply_convert_fusion.25 = bf16[3,512,1536]{2,1,0:T(8,128)(2,1)} fusion(f32[3,512,1536]{2,1,0:T(8,128)} %get-tuple-element.606, f32[3,512,1536]{2,1,0:T(8,128)} %copy-done, f32[3,512]{1,0:T(4,128)S(1)} %get-tuple-element.607), kind=kLoop, calls=%fused_computation.16.clone.1 | loop fusion | flops 7077888 | bytes 23599104 | tf_op jit(solution)/shard_map/while/body/eval_jaxpr/convert_element_type | solution.py:335
  609.2 7.5 multiply_reduce_fusion.7
  616.7 9.4 %multiply_convert_fusion.25 = bf16[3,512,1536]{2,1,0:T(8,128)(2,1)} fusion(f32[3,512,1536]{2,1,0:T(8,128)} %get-tuple-element.606, f32[3,512,1536]{2,1,0:T(8,128)} %copy-done, f32[3,512]{1,0:T(4,128)S(1)} %get-tuple-element.607), kind=kLoop, calls=%fused_computation.16.clone.1 | loop fusion | flops 7077888 | bytes 23599104 | tf_op jit(solution)/shard_map/while/body/eval_jaxpr/convert_element_type | solution.py:335
  652.8 10.0 %convolution_convert_fusion = bf16[8,768,768]{2,1,0:T(8,128)(2,1)S(1)} fusion(bf16[8,480,768]{2,1,0:T(8,128)(2,1)} %fusion.76, f32[8,480]{1,0:T(8,128)S(1)} %copy-done.68, f32[8,480,768]{2,1,0:T(8,128)} %fusion.54), kind=kOutput, calls=%fused_computation.81 | convolution fusion | flops 4569956352 | bytes 27147264 | tf_op jit(solution)/shard_map/ecd,ecf->edf/dot_general | solution.py:272
  679.0 9.0 %convolution_convert_fusion.1 = bf16[8,768,768]{2,1,0:T(8,128)(2,1)S(1)} fusion(bf16[8,480,768]{2,1,0:T(8,128)(2,1)} %fusion.75, bf16[8,480,768]{2,1,0:T(8,128)(2,1)} %fusion.42), kind=kOutput, calls=%fused_computation.82 | convolution fusion | flops 4534566912 | bytes 21233664 | tf_op jit(solution)/shard_map/ecd,ecf->edf/dot_general | solution.py:281
  701.8 8.2 collective-permute-done.36
  714.6 8.1 collective-permute-done.37
  763.2 11.8 %all-to-all-start.2 = ((f32[32,1,624]{2,1,0:T(1,128)}), f32[32,1,624]{2,1,0:T(1,128)S(1)}, u32[]{:S(2)}, u32[]{:S(2)}) async-start(f32[32,1,624]{2,1,0:T(1,128)} %copy.250), calls=%async_computation.2 | async-start | bytes 163840 | tf_op jit(solution)/shard_map/all_to_all | solution.py:385
  789.7 7.3 fusion.131
  797.0 65.3 %reduce-scatter.6.cloned.1.call-done = bf16[9,96,768]{2,1,0:T(8,128)(2,1)} async-done(((bf16[9,768,768]{2,1,0:T(8,128)(2,1)}), bf16[9,96,768]{2,1,0:T(8,128)(2,1)}) %reduce-scatter.6.cloned.1.call-update) | async-done | bytes 1327120 | tf_op jit(solution)/shard_map/reduce_scatter | solution.py:291
  (609 shorter events, 468.7 us)
Async XLA Ops:
  7.2 240.9 %all-gather.5.cloned.1.call-start = ((), (), s32[]{:S(2)}) async-start(), calls=%async_computation.6 | async-start | bytes 1327104 | tf_op jit(solution)/shard_map/all_gather | solution.py:149
  33.7 241.9 %all-gather.7.cloned.1.call-start = ((), (), s32[]{:S(2)}) async-start(), calls=%async_computation.7 | async-start | bytes 11943936 | tf_op jit(solution)/shard_map/all_gather | solution.py:162
  37.1 63.2 %collective-permute-start.25 = (bf16[384,768]{0,1:T(8,128)(2,1)S(1)}, bf16[384,768]{0,1:T(8,128)(2,1)}, u32[]{:S(2)}, u32[]{:S(2)}) collective-permute-start(bf16[384,768]{0,1:T(8,128)(2,1)S(1)} %copy.235), channel_id=1, source_target_pairs={{1,0},{2,1},{3,2},{5,4},{6,5},{7,6},{9,8},{10,9},{11,10},{13,12},{... | collective-permute-start | bytes 1769480 | tf_op jit(solution)/shard_map/ppermute | solution.py:52
  38.6 63.1 %collective-permute-start.24 = (bf16[384,768]{0,1:T(8,128)(2,1)S(1)}, bf16[384,768]{0,1:T(8,128)(2,1)}, u32[]{:S(2)}, u32[]{:S(2)}) collective-permute-start(bf16[384,768]{0,1:T(8,128)(2,1)S(1)} %copy.235), channel_id=1, source_target_pairs={{0,1},{1,2},{2,3},{4,5},{5,6},{6,7},{8,9},{9,10},{10,11},{12,13},{... | collective-permute-start | bytes 1769480 | tf_op jit(solution)/shard_map/ppermute | solution.py:51
  45.3 28.8 %collective-permute-start.1 = (bf16[384,768]{0,1:T(8,128)(2,1)S(1)}, bf16[384,768]{0,1:T(8,128)(2,1)}, u32[]{:S(2)}, u32[]{:S(2)}) collective-permute-start(bf16[384,768]{0,1:T(8,128)(2,1)S(1)} %copy.219), channel_id=1, source_target_pairs={{1,0},{2,1},{3,2},{5,4},{6,5},{7,6},{9,8},{10,9},{11,10},{13,12},{... | collective-permute-start | bytes 1769480 | tf_op jit(solution)/shard_map/ppermute | solution.py:52
  46.6 30.4 %collective-permute-start = (bf16[384,768]{0,1:T(8,128)(2,1)S(1)}, bf16[384,768]{0,1:T(8,128)(2,1)}, u32[]{:S(2)}, u32[]{:S(2)}) collective-permute-start(bf16[384,768]{0,1:T(8,128)(2,1)S(1)} %copy.219), channel_id=1, source_target_pairs={{0,1},{1,2},{2,3},{4,5},{5,6},{6,7},{8,9},{9,10},{10,11},{12,13},{... | collective-permute-start | bytes 1769480 | tf_op jit(solution)/shard_map/ppermute | solution.py:51
  70.7 24.6 %all-to-all-start = ((f32[32,1,624]{2,1,0:T(1,128)}), f32[32,1,624]{2,1,0:T(1,128)}, u32[]{:S(2)}, u32[]{:S(2)}) async-start(f32[32,1,624]{2,1,0:T(1,128)} %all_to_all.19), calls=%async_computation | async-start | bytes 163840 | tf_op jit(solution)/shard_map/all_to_all | solution.py:171
  74.0 216.1 %all-gather.9.cloned.1.call-start = ((), (), s32[]{:S(2)}) async-start(), calls=%async_computation.8 | async-start | bytes 11943936 | tf_op jit(solution)/shard_map/all_gather | solution.py:161
  77.0 20.8 %collective-permute-start.4 = (bf16[384,768]{0,1:T(8,128)(2,1)}, bf16[384,768]{0,1:T(8,128)(2,1)}, u32[]{:S(2)}, u32[]{:S(2)}) collective-permute-start(bf16[384,768]{0,1:T(8,128)(2,1)} %collective-permute-done), channel_id=1, source_target_pairs={{1,2},{2,3},{5,6},{6,7},{9,10},{10,11},{13,14},{14,15},{17,18},{18... | collective-permute-start | bytes 1769480 | tf_op jit(solution)/shard_map/ppermute | solution.py:51
  100.4 73.9 %collective-permute-start.26 = (bf16[384,768]{0,1:T(8,128)(2,1)}, bf16[384,768]{0,1:T(8,128)(2,1)}, u32[]{:S(2)}, u32[]{:S(2)}) collective-permute-start(bf16[384,768]{0,1:T(8,128)(2,1)} %collective-permute-done.25), channel_id=1, source_target_pairs={{1,0},{2,1},{5,4},{6,5},{9,8},{10,9},{13,12},{14,13},{17,16},{18,1... | collective-permute-start | bytes 1769480 | tf_op jit(solution)/shard_map/ppermute | solution.py:52
  101.7 75.6 %collective-permute-start.28 = (bf16[384,768]{0,1:T(8,128)(2,1)}, bf16[384,768]{0,1:T(8,128)(2,1)}, u32[]{:S(2)}, u32[]{:S(2)}) collective-permute-start(bf16[384,768]{0,1:T(8,128)(2,1)} %collective-permute-done.24), channel_id=1, source_target_pairs={{1,2},{2,3},{5,6},{6,7},{9,10},{10,11},{13,14},{14,15},{17,18},{18... | collective-permute-start | bytes 1769480 | tf_op jit(solution)/shard_map/ppermute | solution.py:51
  174.2 29.8 %collective-permute-start.27 = (bf16[384,768]{0,1:T(8,128)(2,1)}, bf16[384,768]{0,1:T(8,128)(2,1)}, u32[]{:S(2)}, u32[]{:S(2)}) collective-permute-start(bf16[384,768]{0,1:T(8,128)(2,1)} %collective-permute-done.26), channel_id=1, source_target_pairs={{1,0},{5,4},{9,8},{13,12},{17,16},{21,20},{25,24},{29,28}} | collective-permute-start | bytes 1769480 | tf_op jit(solution)/shard_map/ppermute | solution.py:52
  177.3 30.8 %collective-permute-start.29 = (bf16[384,768]{0,1:T(8,128)(2,1)}, bf16[384,768]{0,1:T(8,128)(2,1)}, u32[]{:S(2)}, u32[]{:S(2)}) collective-permute-start(bf16[384,768]{0,1:T(8,128)(2,1)} %collective-permute-done.28), channel_id=1, source_target_pairs={{2,3},{6,7},{10,11},{14,15},{18,19},{22,23},{26,27},{30,31}} | collective-permute-start | bytes 1769480 | tf_op jit(solution)/shard_map/ppermute | solution.py:51
  182.3 27.8 %collective-permute-start.6 = (bf16[1536,192]{0,1:T(8,128)(2,1)}, bf16[1536,192]{0,1:T(8,128)(2,1)S(1)}, u32[]{:S(2)}, u32[]{:S(2)}) collective-permute-start(bf16[1536,192]{0,1:T(8,128)(2,1)} %bitcast.64), channel_id=1, source_target_pairs={{0,1},{1,2},{2,3},{4,5},{5,6},{6,7},{8,9},{9,10},{10,11},{12,13},{... | collective-permute-start | bytes 1769480 | tf_op jit(solution)/shard_map/ppermute | solution.py:51
  191.4 23.7 %collective-permute-start.8 = (bf16[1536,192]{0,1:T(8,128)(2,1)}, bf16[1536,192]{0,1:T(8,128)(2,1)S(1)}, u32[]{:S(2)}, u32[]{:S(2)}) collective-permute-start(bf16[1536,192]{0,1:T(8,128)(2,1)} %collective-permute-done.7), channel_id=1, source_target_pairs={{1,0},{2,1},{5,4},{6,5},{9,8},{10,9},{13,12},{14,13},{17,16},{18,1... | collective-permute-start | bytes 1769480 | tf_op jit(solution)/shard_map/ppermute | solution.py:52
  210.1 25.1 %collective-permute-start.10 = (bf16[1536,192]{0,1:T(8,128)(2,1)S(1)}, bf16[1536,192]{0,1:T(8,128)(2,1)S(1)}, u32[]{:S(2)}, u32[]{:S(2)}) collective-permute-start(bf16[1536,192]{0,1:T(8,128)(2,1)S(1)} %collective-permute-done.6), channel_id=1, source_target_pairs={{1,2},{2,3},{5,6},{6,7},{9,10},{10,11},{13,14},{14,15},{17,18},{18... | collective-permute-start | bytes 1769480 | tf_op jit(solution)/shard_map/ppermute | solution.py:51
  215.1 20.8 %collective-permute-start.9 = (bf16[1536,192]{0,1:T(8,128)(2,1)S(1)}, bf16[1536,192]{0,1:T(8,128)(2,1)S(1)}, u32[]{:S(2)}, u32[]{:S(2)}) collective-permute-start(bf16[1536,192]{0,1:T(8,128)(2,1)S(1)} %collective-permute-done.8), channel_id=1, source_target_pairs={{1,0},{5,4},{9,8},{13,12},{17,16},{21,20},{25,24},{29,28}} | collective-permute-start | bytes 1769480 | tf_op jit(solution)/shard_map/ppermute | solution.py:52
  376.5 38.9 %collective-permute-start.30 = (bf16[384,768]{0,1:T(8,128)(2,1)}, bf16[384,768]{0,1:T(8,128)(2,1)}, u32[]{:S(2)}, u32[]{:S(2)}) collective-permute-start(bf16[384,768]{0,1:T(8,128)(2,1)} %get-tuple-element.461), channel_id=1, source_target_pairs={{0,1},{4,5},{8,9},{12,13},{16,17},{20,21},{24,25},{28,29}} | collective-permute-start | bytes 1769480 | tf_op jit(solution)/shard_map/ppermute | solution.py:77
  413.9 20.7 %collective-permute-start.33 = (bf16[384,768]{0,1:T(8,128)(2,1)}, bf16[384,768]{0,1:T(8,128)(2,1)}, u32[]{:S(2)}, u32[]{:S(2)}) collective-permute-start(bf16[384,768]{0,1:T(8,128)(2,1)} %get-tuple-element.462), channel_id=1, source_target_pairs={{3,2},{7,6},{11,10},{15,14},{19,18},{23,22},{27,26},{31,30}} | collective-permute-start | bytes 1769480 | tf_op jit(solution)/shard_map/ppermute | solution.py:78
  417.5 22.3 %collective-permute-start.31 = (bf16[384,768]{0,1:T(8,128)(2,1)}, bf16[384,768]{0,1:T(8,128)(2,1)}, u32[]{:S(2)}, u32[]{:S(2)}) collective-permute-start(bf16[384,768]{0,1:T(8,128)(2,1)} %add_convert_fusion.8), channel_id=1, source_target_pairs={{0,1},{1,2},{4,5},{5,6},{8,9},{9,10},{12,13},{13,14},{16,17},{17,1... | collective-permute-start | bytes 1769480 | tf_op jit(solution)/shard_map/ppermute | solution.py:77
  419.6 22.6 %collective-permute-start.21 = (bf16[384,768]{0,1:T(8,128)(2,1)S(1)}, bf16[384,768]{0,1:T(8,128)(2,1)}, u32[]{:S(2)}, u32[]{:S(2)}) collective-permute-start(bf16[384,768]{0,1:T(8,128)(2,1)S(1)} %get-tuple-element.466), channel_id=1, source_target_pairs={{3,2},{7,6},{11,10},{15,14},{19,18},{23,22},{27,26},{31,30}} | collective-permute-start | bytes 1769480 | tf_op jit(solution)/shard_map/ppermute | solution.py:78
  429.4 20.4 %collective-permute-start.19 = (bf16[384,768]{0,1:T(8,128)(2,1)}, bf16[384,768]{0,1:T(8,128)(2,1)}, u32[]{:S(2)}, u32[]{:S(2)}) collective-permute-start(bf16[384,768]{0,1:T(8,128)(2,1)} %add_convert_fusion.13), channel_id=1, source_target_pairs={{0,1},{1,2},{4,5},{5,6},{8,9},{9,10},{12,13},{13,14},{16,17},{17,1... | collective-permute-start | bytes 1769480 | tf_op jit(solution)/shard_map/ppermute | solution.py:77
  441.4 20.8 %collective-permute-start.34 = (bf16[384,768]{0,1:T(8,128)(2,1)S(1)}, bf16[384,768]{0,1:T(8,128)(2,1)S(1)}, u32[]{:S(2)}, u32[]{:S(2)}) collective-permute-start(bf16[384,768]{0,1:T(8,128)(2,1)S(1)} %get-tuple-element.460), channel_id=1, source_target_pairs={{2,1},{3,2},{6,5},{7,6},{10,9},{11,10},{14,13},{15,14},{18,17},{19... | collective-permute-start | bytes 1769480 | tf_op jit(solution)/shard_map/ppermute | solution.py:78
  457.6 22.8 %collective-permute-start.20 = (bf16[384,768]{0,1:T(8,128)(2,1)S(1)}, bf16[384,768]{0,1:T(8,128)(2,1)S(1)}, u32[]{:S(2)}, u32[]{:S(2)}) collective-permute-start(bf16[384,768]{0,1:T(8,128)(2,1)S(1)} %get-tuple-element.463), channel_id=1, source_target_pairs={{0,1},{1,2},{2,3},{4,5},{5,6},{6,7},{8,9},{9,10},{10,11},{12,13},{... | collective-permute-start | bytes 1769480 | tf_op jit(solution)/shard_map/ppermute | solution.py:77
  464.0 24.9 %collective-permute-start.23 = (bf16[384,768]{0,1:T(8,128)(2,1)S(1)}, bf16[384,768]{0,1:T(8,128)(2,1)S(1)}, u32[]{:S(2)}, u32[]{:S(2)}) collective-permute-start(bf16[384,768]{0,1:T(8,128)(2,1)S(1)} %add_convert_fusion.10), channel_id=1, source_target_pairs={{1,0},{2,1},{3,2},{5,4},{6,5},{7,6},{9,8},{10,9},{11,10},{13,12},{... | collective-permute-start | bytes 1769480 | tf_op jit(solution)/shard_map/ppermute | solution.py:78
  505.5 28.0 %all-to-all-start.1 = ((bf16[4,384,192]{1,2,0:T(8,128)(2,1)}), bf16[4,384,192]{1,2,0:T(8,128)(2,1)}, u32[]{:S(2)}, u32[]{:S(2)}) async-start(bf16[4,384,192]{1,2,0:T(8,128)(2,1)} %bitcast.27), calls=%async_computation.1 | async-start | bytes 1179648 | tf_op jit(solution)/shard_map/all_to_all | solution.py:313
  509.7 235.1 %reduce-scatter.10.cloned.1.call-start = ((), (), s32[]{:S(2)}) async-start(), calls=%async_computation.11 | async-start | bytes 1327104
  525.4 121.9 %collective-permute-start.44 = (bf16[768,192]{0,1:T(8,128)(2,1)}, bf16[768,192]{0,1:T(8,128)(2,1)}, u32[]{:S(2)}, u32[]{:S(2)}) collective-permute-start(bf16[768,192]{0,1:T(8,128)(2,1)} %get-tuple-element.472), channel_id=1, source_target_pairs={{0,1},{1,2},{2,3},{4,5},{5,6},{6,7},{8,9},{9,10},{10,11},{12,13},{... | collective-permute-start | bytes 884744 | tf_op jit(solution)/shard_map/ppermute | solution.py:77
  532.1 108.2 %collective-permute-start.46 = (bf16[768,192]{0,1:T(8,128)(2,1)}, bf16[768,192]{0,1:T(8,128)(2,1)}, u32[]{:S(2)}, u32[]{:S(2)}) collective-permute-start(bf16[768,192]{0,1:T(8,128)(2,1)} %get-tuple-element.473), channel_id=1, source_target_pairs={{2,1},{3,2},{6,5},{7,6},{10,9},{11,10},{14,13},{15,14},{18,17},{19... | collective-permute-start | bytes 884744 | tf_op jit(solution)/shard_map/ppermute | solution.py:78
  652.7 132.7 %reduce-scatter.8.cloned.1.call-start = ((), (), s32[]{:S(2)}) async-start(), calls=%async_computation.10 | async-start | bytes 11943936 | tf_op jit(solution)/shard_map/reduce_scatter | solution.py:290
  673.7 188.6 %reduce-scatter.6.cloned.1.call-start = ((), (), s32[]{:S(2)}) async-start(), calls=%async_computation.9 | async-start | bytes 11943936 | tf_op jit(solution)/shard_map/reduce_scatter | solution.py:291
  725.1 24.5 %collective-permute-start.38 = (bf16[384,768]{0,1:T(8,128)(2,1)}, bf16[384,768]{0,1:T(8,128)(2,1)}, u32[]{:S(2)}, u32[]{:S(2)}) collective-permute-start(bf16[384,768]{0,1:T(8,128)(2,1)} %get-tuple-element.455), channel_id=1, source_target_pairs={{0,1},{1,2},{2,3},{4,5},{5,6},{6,7},{8,9},{9,10},{10,11},{12,13},{... | collective-permute-start | bytes 1769480 | tf_op jit(solution)/shard_map/ppermute | solution.py:77
  (163 other events, 2756.1 us)
Sparse Core Ops, SparseCore 0:
  33.8 22.2 all-gather.4
  58.6 66.1 all-gather.6
  126.7 63.8 all-gather.8
  652.8 37.5 reduce-scatter.9
  694.1 82.1 reduce-scatter.7
  780.1 82.1 reduce-scatter.5

commit v2 on v1

v2 whole, which is shorter than its diff:
```python
import functools
import math

import jax
import jax.numpy as jnp
from jax import lax
from jax.experimental import pallas as pl
from jax.experimental.pallas import tpu as pltpu
from jax.sharding import PartitionSpec as P

H = 12
HD = 64
E = 8
STEP = 10

beta_one = 0.9
beta_two = 0.95
epsilon = 1e-08
weight_decay = 0.1
norm_floor = 1e-06
highest = lax.Precision.HIGHEST
f32 = jnp.float32
bf16 = jnp.bfloat16


def norm_parts(values):
    centred = values - jnp.mean(values, axis=1, keepdims=True)
    inverse = lax.rsqrt(jnp.mean(centred * centred, axis=1, keepdims=True) + norm_floor)
    return centred * inverse, inverse


def norm_back(normed, inverse, gradient):
    first = jnp.mean(gradient, axis=1, keepdims=True)
    second = jnp.mean(gradient * normed, axis=1, keepdims=True)
    return inverse * (gradient - first - normed * second)


def after(values, *earlier):
    return lax.optimization_barrier((values, earlier))[0]


class Gather:
    def __init__(self, block):
        self.ups, self.downs = [block], [block]

    def send(self):
        width, step = lax.axis_size("mp"), len(self.ups)
        up_pairs = [(i, i + 1) for i in range(step - 1, width - 1)]
        down_pairs = [(i + 1, i) for i in range(width - step)]
        return (
            lax.ppermute(self.ups[-1], "mp", up_pairs),
            lax.ppermute(self.downs[-1], "mp", down_pairs),
        )

    def take(self, pair):
        self.ups.append(pair[0])
        self.downs.append(pair[1])

    def blocks(self):
        width, rank = lax.axis_size("mp"), lax.axis_index("mp")
        pairs = zip(range(1, width), self.ups[1:], reversed(self.downs[1:]))
        return [self.ups[0]] + [jnp.where(rank >= i, u, d) for i, u, d in pairs]

    def whole(self, axis=0):
        width, rank = lax.axis_size("mp"), lax.axis_index("mp")
        return jnp.concatenate(
            [
                functools.reduce(
                    lambda kept, r: jnp.where(rank == r, self.block_of(index, r), kept),
                    range(1, width),
                    self.block_of(index, 0),
                )
                for index in range(width)
            ],
            axis=axis,
        )

    def block_of(self, index, rank):
        return self.ups[rank - index] if rank >= index else self.downs[index - rank]


class Scatter:
    def __init__(self, partial, axis=0):
        self.partial, self.axis, self.step = partial, axis, 1
        self.up, self.down = None, None

    def part(self, offset):
        width, rank = lax.axis_size("mp"), lax.axis_index("mp")
        extent = self.partial.shape[self.axis] // width
        index = jnp.clip(rank + offset, 0, width - 1)
        return lax.dynamic_slice_in_dim(self.partial, index * extent, extent, self.axis)

    def send(self):
        width, step = lax.axis_size("mp"), self.step
        up, down = self.part(width - step), self.part(step - width)
        if self.up is not None:
            up = (up.astype(f32) + self.up.astype(f32)).astype(bf16)
            down = (down.astype(f32) + self.down.astype(f32)).astype(bf16)
        return (
            lax.ppermute(up, "mp", [(i, i + 1) for i in range(step)]),
            lax.ppermute(down, "mp", [(i, i - 1) for i in range(width - step, width)]),
        )

    def take(self, pair):
        self.up, self.down = pair
        self.step += 1

    def terms(self):
        return self.part(0), self.up, self.down

    def total(self):
        return sum(t.astype(f32) for t in self.terms())


def phase(transfers, work):
    pairs, work = lax.optimization_barrier(([t.send() for t in transfers], work))
    for transfer, pair in zip(transfers, pairs):
        transfer.take(pair)
    return work


LANES = 128
Q_BLOCK = 256
FAR = 2.0**50
NT = (((1,), (1,)), ((), ()))
TN = (((0,), (0,)), ((), ()))
NN = (((1,), (0,)), ((), ()))


def dot(a, b, dims=NN):
    return lax.dot_general(a, b, dims, preferred_element_type=f32)


def key_widths(group):
    return sorted({min(w, group) for w in (512, 768, 1024, group)})


def key_windows(lengths, group):
    ends = jnp.cumsum(lengths)
    begins = ends - lengths
    first = jnp.arange(group // Q_BLOCK, dtype=jnp.int32) * Q_BLOCK
    last = first + Q_BLOCK - 1
    low = jnp.max(jnp.where(begins[None, :] <= first[:, None], begins[None, :], 0), axis=1)
    high = jnp.min(jnp.where(ends[None, :] > last[:, None], ends[None, :], group), axis=1)
    low = low // LANES * LANES
    widths = jnp.array(key_widths(group), jnp.int32)
    kind = jnp.sum((high - low)[:, None] > widths[None, :], axis=1).astype(jnp.int32)
    return jnp.minimum(low, group - widths[kind]).astype(jnp.int32), kind


def attend_kernel(start_ref, kind_ref, qkv_ref, mixed_ref, log_ref, *, group):
    block = pl.program_id(1)
    rows = pl.ds(pl.multiple_of(block * Q_BLOCK, Q_BLOCK), Q_BLOCK)
    query = qkv_ref[rows, 0:LANES] * jnp.asarray(HD**-0.5, bf16)
    for index, extent in enumerate(key_widths(group)):

        @pl.when(kind_ref[block] == index)
        def _():
            keys = pl.ds(pl.multiple_of(start_ref[block], LANES), extent)
            scores = dot(qkv_ref[keys, LANES : 2 * LANES], query, NT)
            peak = jnp.max(scores, axis=0, keepdims=True)
            exps = jnp.exp(scores - peak)
            total = jnp.sum(exps, axis=0, keepdims=True)
            probs = (exps * (1.0 / total)).astype(bf16)
            mixed = dot(qkv_ref[keys, 2 * LANES : 3 * LANES], probs, TN)
            mixed_ref[...] = mixed[:HD].astype(bf16)
            log_ref[...] = (peak + jnp.log(total))[None]


def attend(qkv, start, kind):
    group = qkv.shape[0]
    heads = qkv.shape[1] // (3 * LANES)
    blocks = group // Q_BLOCK
    return pl.pallas_call(
        functools.partial(attend_kernel, group=group),
        out_shape=(
            jax.ShapeDtypeStruct((heads * HD, group), bf16),
            jax.ShapeDtypeStruct((heads, 1, group), f32),
        ),
        grid_spec=pltpu.PrefetchScalarGridSpec(
            num_scalar_prefetch=2,
            grid=(heads, blocks),
            in_specs=[pl.BlockSpec((group, 3 * LANES), lambda h, i, *_: (0, h))],
            out_specs=(
                pl.BlockSpec((HD, Q_BLOCK), lambda h, i, *_: (h, i)),
                pl.BlockSpec((1, 1, Q_BLOCK), lambda h, i, *_: (h, 0, i)),
            ),
        ),
        compiler_params=pltpu.CompilerParams(vmem_limit_bytes=40 * 2**20),
        cost_estimate=pl.CostEstimate(
            flops=16 * heads * group * group * HD, bytes_accessed=6 * 2**20, transcendentals=heads * group * group
        ),
        name="attend",
    )(start, kind, qkv)


def attend_back_kernel(
    start_ref, kind_ref, qkv_ref, grad_ref, log_ref, out_ref, key_total, value_total, *, group
):
    block = pl.program_id(1)

    @pl.when(block == 0)
    def _():
        key_total[...] = jnp.zeros_like(key_total)
        value_total[...] = jnp.zeros_like(value_total)

    rows = pl.ds(pl.multiple_of(block * Q_BLOCK, Q_BLOCK), Q_BLOCK)
    scaling = HD**-0.5
    query = qkv_ref[rows, 0:LANES] * jnp.asarray(scaling, bf16)
    grad = grad_ref[...]
    kept = lax.broadcasted_iota(jnp.int32, (1, LANES), 1) < HD
    for index, extent in enumerate(key_widths(group)):

        @pl.when(kind_ref[block] == index)
        def _():
            keys = pl.ds(pl.multiple_of(start_ref[block], LANES), extent)
            key_rows = qkv_ref[keys, LANES : 2 * LANES]
            value_rows = qkv_ref[keys, 2 * LANES : 3 * LANES]
            probs = jnp.exp(dot(key_rows, query, NT) - log_ref[0])
            grad_probs = dot(value_rows[:, :HD], grad)
            middle = jnp.sum(probs * grad_probs, axis=0, keepdims=True)
            grad_scores = (probs * (grad_probs - middle)).astype(bf16)
            value_total[keys, :HD] += dot(probs.astype(bf16), grad, NT)
            key_total[keys, :] += dot(grad_scores, query)
            grad_query = dot(key_rows, grad_scores, TN).T * scaling
            out_ref[rows, 0:LANES] = jnp.where(kept, grad_query, 0.0).astype(bf16)

    @pl.when(block == pl.num_programs(1) - 1)
    def _():
        out_ref[:, LANES : 2 * LANES] = jnp.where(kept, key_total[...], 0.0).astype(bf16)
        out_ref[:, 2 * LANES : 3 * LANES] = value_total[...].astype(bf16)


def attend_back(qkv, grad_mixed, logs, start, kind):
    group = qkv.shape[0]
    heads = qkv.shape[1] // (3 * LANES)
    blocks = group // Q_BLOCK
    return pl.pallas_call(
        functools.partial(attend_back_kernel, group=group),
        out_shape=jax.ShapeDtypeStruct(qkv.shape, bf16),
        grid_spec=pltpu.PrefetchScalarGridSpec(
            num_scalar_prefetch=2,
            grid=(heads, blocks),
            in_specs=[
                pl.BlockSpec((group, 3 * LANES), lambda h, i, *_: (0, h)),
                pl.BlockSpec((HD, Q_BLOCK), lambda h, i, *_: (h, i)),
                pl.BlockSpec((1, 1, Q_BLOCK), lambda h, i, *_: (h, 0, i)),
            ],
            out_specs=pl.BlockSpec((group, 3 * LANES), lambda h, i, *_: (0, h)),
            scratch_shapes=[pltpu.VMEM((group, LANES), f32), pltpu.VMEM((group, LANES), f32)],
        ),
        compiler_params=pltpu.CompilerParams(vmem_limit_bytes=40 * 2**20),
        cost_estimate=pl.CostEstimate(
            flops=40 * heads * group * group * HD, bytes_accessed=12 * 2**20, transcendentals=heads * group * group
        ),
        name="attend_back",
    )(start, kind, qkv, grad_mixed, logs)


def item_rows(table_ref, term, width, segment, items):
    columns = slice(term * width, (term + 1) * width)
    rows = table_ref[0:1, columns]
    for item in range(1, items):
        rows = jnp.where(segment >= item, table_ref[item : item + 1, columns], rows)
    return rows


def item_sums(values, segment, items):
    return jnp.concatenate(
        [jnp.sum(jnp.where(segment == item, values, 0.0), axis=0, keepdims=True) for item in range(items)], axis=0
    )


def norm_one_kernel(*refs, width_mp, items):
    rank_ref, segment_ref, table_ref = refs[:3]
    block_refs, (rows_ref, h_ref) = refs[3 : 3 + width_mp], refs[3 + width_mp :]
    step = pl.program_id(0)
    segment = segment_ref[...]
    width = rows_ref.shape[1]
    for place in range(width_mp):

        @pl.when(step == place)
        def _():
            rows = block_refs[place][...]
            rows_ref[...] = rows
            normed, _ = norm_parts(rows.astype(f32))
            shift = item_rows(table_ref, 0, width, segment, items)
            scale = item_rows(table_ref, 1, width, segment, items)
            h_ref[...] = (normed * (1.0 + scale) + shift).astype(bf16)


def norm_one(blocks, table, segment):
    width_mp, (rows, width) = len(blocks), blocks[0].shape
    group, items = rows * width_mp, table.shape[0]

    def placed(i, rank):
        return (lax.rem(rank[0] - i + width_mp, width_mp), 0)

    def plain(*shape):
        return pl.BlockSpec(shape, lambda i, rank: (0,) * len(shape))

    return pl.pallas_call(
        functools.partial(norm_one_kernel, width_mp=width_mp, items=items),
        out_shape=(jax.ShapeDtypeStruct((group, width), bf16),) * 2,
        grid_spec=pltpu.PrefetchScalarGridSpec(
            num_scalar_prefetch=1,
            grid=(width_mp,),
            in_specs=[pl.BlockSpec((rows, 1), placed), plain(*table.shape)]
            + [plain(rows, width)] * width_mp,
            out_specs=(pl.BlockSpec((rows, width), placed),) * 2,
        ),
        compiler_params=pltpu.CompilerParams(vmem_limit_bytes=40 * 2**20),
        cost_estimate=pl.CostEstimate(flops=2 * 10**7, bytes_accessed=8 * 2**20, transcendentals=0),
        name="norm_one",
    )(lax.axis_index("mp").reshape(1), segment, table, *blocks)


def norm_two_kernel(*refs, width_mp, items):
    rank_ref, segment_ref, table_ref, rows_ref, proj_ref = refs[:5]
    mixed_refs = refs[5 : 5 + width_mp]
    h_ref, x_mine_ref, attn_mine_ref, mixed_mine_ref = refs[5 + width_mp :]
    step = pl.program_id(0)
    rank = rank_ref[0]
    segment = segment_ref[...]
    width = rows_ref.shape[1]
    heads = mixed_refs[0].shape[0]
    attn = jnp.zeros(rows_ref.shape, f32)
    for place in range(width_mp):
        owner = lax.rem(rank - place + width_mp, width_mp)
        here = pl.ds(pl.multiple_of(owner * heads, heads), heads)
        mixed = mixed_refs[place][...]
        attn += dot(mixed, proj_ref[here, :], TN)

        @pl.when(step == rank)
        def _():
            mixed_mine_ref[here, :] = mixed

    x_one = rows_ref[...].astype(f32) + item_rows(table_ref, 2, width, segment, items) * attn

    @pl.when(step == rank)
    def _():
        x_mine_ref[...] = x_one
        attn_mine_ref[...] = attn

    normed, _ = norm_parts(x_one)
    shift = item_rows(table_ref, 3, width, segment, items)
    scale = item_rows(table_ref, 4, width, segment, items)
    h_ref[...] = (normed * (1.0 + scale) + shift).astype(bf16)


def norm_two(blocks, patches, proj, table, segment):
    width_mp, (heads, group) = len(blocks), blocks[0].shape
    rows, width, items = group // width_mp, patches.shape[1], table.shape[0]

    def plain(*shape):
        return pl.BlockSpec(shape, lambda i, rank: (0,) * len(shape))

    return pl.pallas_call(
        functools.partial(norm_two_kernel, width_mp=width_mp, items=items),
        out_shape=(
            jax.ShapeDtypeStruct((group, width), bf16),
            jax.ShapeDtypeStruct((rows, width), f32),
            jax.ShapeDtypeStruct((rows, width), f32),
            jax.ShapeDtypeStruct((heads * width_mp, rows), bf16),
        ),
        grid_spec=pltpu.PrefetchScalarGridSpec(
            num_scalar_prefetch=1,
            grid=(width_mp,),
            in_specs=[
                pl.BlockSpec((rows, 1), lambda i, rank: (i, 0)),
                plain(*table.shape),
                pl.BlockSpec((rows, width), lambda i, rank: (i, 0)),
                plain(*proj.shape),
            ]
            + [pl.BlockSpec((heads, rows), lambda i, rank: (0, i))] * width_mp,
            out_specs=(
                pl.BlockSpec((rows, width), lambda i, rank: (i, 0)),
                plain(rows, width),
                plain(rows, width),
                plain(heads * width_mp, rows),
            ),
        ),
        compiler_params=pltpu.CompilerParams(vmem_limit_bytes=40 * 2**20),
        cost_estimate=pl.CostEstimate(flops=2 * 10**9, bytes_accessed=13 * 2**20, transcendentals=0),
        name="norm_two",
    )(lax.axis_index("mp").reshape(1), segment, table, patches, proj, *blocks)


def back_two_kernel(
    segment_ref,
    table_ref,
    own_ref,
    up_ref,
    down_ref,
    x_ref,
    attn_ref,
    cot_ref,
    proj_ref,
    grad_x_ref,
    grad_attn_ref,
    grad_mixed_ref,
    sums_ref,
    *,
    items,
):
    segment = segment_ref[...]
    width = x_ref.shape[1]
    grad = own_ref[...].astype(f32) + up_ref[...].astype(f32) + down_ref[...].astype(f32)
    normed, inverse = norm_parts(x_ref[...])
    scale = item_rows(table_ref, 4, width, segment, items)
    grad_x = cot_ref[...].astype(f32) + norm_back(normed, inverse, grad * (1.0 + scale))
    grad_x_ref[...] = grad_x
    grad_attn = (item_rows(table_ref, 2, width, segment, items) * grad_x).astype(bf16)
    grad_attn_ref[...] = grad_attn
    grad_mixed_ref[...] = dot(proj_ref[...], grad_attn, NT).astype(bf16)
    sums_ref[:, 0:width] = item_sums(grad_x * attn_ref[...], segment, items)
    sums_ref[:, width : 2 * width] = item_sums(grad, segment, items)
    sums_ref[:, 2 * width :] = item_sums(grad * normed, segment, items)


def back_two(terms, x_one, attn, cotangent, proj, table, segment):
    rows, width = x_one.shape
    items = table.shape[0]
    return pl.pallas_call(
        functools.partial(back_two_kernel, items=items),
        out_shape=(
            jax.ShapeDtypeStruct((rows, width), f32),
            jax.ShapeDtypeStruct((rows, width), bf16),
            jax.ShapeDtypeStruct((proj.shape[0], rows), bf16),
            jax.ShapeDtypeStruct((items, 3 * width), f32),
        ),
        compiler_params=pltpu.CompilerParams(vmem_limit_bytes=40 * 2**20),
        cost_estimate=pl.CostEstimate(flops=10**9, bytes_accessed=9 * 2**20, transcendentals=0),
        name="back_two",
    )(segment, table, *terms, x_one, attn, cotangent, proj)


def back_one_kernel(
    segment_ref,
    table_ref,
    own_ref,
    up_ref,
    down_ref,
    patches_ref,
    grad_x_ref,
    grad_ref,
    sums_ref,
    *,
    items,
):
    segment = segment_ref[...]
    width = patches_ref.shape[1]
    grad = own_ref[...].astype(f32) + up_ref[...].astype(f32) + down_ref[...].astype(f32)
    normed, inverse = norm_parts(patches_ref[...].astype(f32))
    scale = item_rows(table_ref, 1, width, segment, items)
    grad_ref[...] = (grad_x_ref[...] + norm_back(normed, inverse, grad * (1.0 + scale))).astype(bf16)
    sums_ref[:, 0:width] = item_sums(grad, segment, items)
    sums_ref[:, width:] = item_sums(grad * normed, segment, items)


def back_one(terms, patches, grad_x, table, segment):
    rows, width = patches.shape
    items = table.shape[0]
    return pl.pallas_call(
        functools.partial(back_one_kernel, items=items),
        out_shape=(
            jax.ShapeDtypeStruct((rows, width), bf16),
            jax.ShapeDtypeStruct((items, 2 * width), f32),
        ),
        compiler_params=pltpu.CompilerParams(vmem_limit_bytes=40 * 2**20),
        cost_estimate=pl.CostEstimate(flops=10**7, bytes_accessed=5 * 2**20, transcendentals=0),
        name="back_one",
    )(segment, table, *terms, patches, grad_x)


def outcome_kernel(
    segment_ref, table_ref, own_ref, up_ref, down_ref, x_ref, cot_ref, out_ref, sums_ref, *, items
):
    segment = segment_ref[...]
    width = x_ref.shape[1]
    branch = own_ref[...].astype(f32) + up_ref[...].astype(f32) + down_ref[...].astype(f32)
    gate = item_rows(table_ref, 5, width, segment, items)
    out_ref[...] = (x_ref[...] + gate * branch).astype(bf16)
    sums_ref[...] = item_sums(cot_ref[...].astype(f32) * branch, segment, items)


def outcome(terms, x_one, cotangent, table, segment):
    rows, width = x_one.shape
    items = table.shape[0]
    return pl.pallas_call(
        functools.partial(outcome_kernel, items=items),
        out_shape=(
            jax.ShapeDtypeStruct((rows, width), bf16),
            jax.ShapeDtypeStruct((items, width), f32),
        ),
        compiler_params=pltpu.CompilerParams(vmem_limit_bytes=40 * 2**20),
        cost_estimate=pl.CostEstimate(flops=10**7, bytes_accessed=5 * 2**20, transcendentals=0),
        name="outcome",
    )(segment, table, *terms, x_one, cotangent)


def gelu_terms(before):
    slope = (2.0 / math.pi) ** 0.5
    square = before * before
    curve = jnp.tanh(slope * before * (1.0 + 0.044715 * square))
    half = 0.5 * (1.0 + curve)
    value = before * half
    derivative = half + (0.5 * slope) * before * (1.0 - curve * curve) * (1.0 + 0.134145 * square)
    return value, derivative


def slot_picks(place_row, capacity):
    slots = lax.broadcasted_iota(jnp.int32, (capacity, place_row.shape[1]), 0)
    return slots == place_row


def row_chunks(group):
    return [slice(first, first + 512) for first in range(0, group, 512)]


def before_kernel(
    place_ref, named_ref, branch_ref, weight_ref, slots_ref, named_slots_ref, back_ref, shared_ref, *, experts
):
    step = pl.program_id(0)

    @pl.when(step < experts)
    def _():
        picks = slot_picks(place_ref[0], slots_ref.shape[1]).astype(bf16)
        slots = dot(picks, branch_ref[...]).astype(bf16)
        slots_ref[0] = slots
        named_slots_ref[0] = dot(picks, named_ref[...]).astype(bf16)
        back_ref[0] = dot(slots, weight_ref[0]).astype(bf16)

    @pl.when(step == experts)
    def _():
        for chunk in row_chunks(shared_ref.shape[0]):
            shared_ref[chunk, :] = dot(branch_ref[chunk, :], weight_ref[0]).astype(bf16)


def whole(*shape):
    return pl.BlockSpec(shape, lambda *_: (0,) * len(shape))


def per_expert(experts, *shape):
    return pl.BlockSpec(
        (1,) + shape, lambda e, *_: (jnp.minimum(e, experts - 1),) + (0,) * len(shape)
    )


def per_slab(*shape):
    return pl.BlockSpec((1,) + shape, lambda e, *_: (e,) + (0,) * len(shape))


def experts_before(places, named, branch, out_t, capacity):
    group, width = branch.shape
    experts, hidden = out_t.shape[0] - 1, out_t.shape[2]
    return pl.pallas_call(
        functools.partial(before_kernel, experts=experts),
        out_shape=(
            jax.ShapeDtypeStruct((experts, capacity, width), bf16),
            jax.ShapeDtypeStruct((experts, capacity, LANES), bf16),
            jax.ShapeDtypeStruct((experts, capacity, hidden), bf16),
            jax.ShapeDtypeStruct((group, hidden), bf16),
        ),
        grid=(experts + 1,),
        in_specs=[
            per_expert(experts, 1, group),
            whole(group, LANES),
            whole(group, width),
            per_slab(width, hidden),
        ],
        out_specs=(
            per_expert(experts, capacity, width),
            per_expert(experts, capacity, LANES),
            per_expert(experts, capacity, hidden),
            whole(group, hidden),
        ),
        compiler_params=pltpu.CompilerParams(vmem_limit_bytes=48 * 2**20),
        cost_estimate=pl.CostEstimate(
            flops=16 * 10**9, bytes_accessed=30 * 2**20, transcendentals=0
        ),
        name="experts_before",
    )(places.reshape(experts, 1, group), named, branch, out_t)


def slots_of(picked, slots):
    index = lax.broadcasted_iota(jnp.int32, (picked.shape[0], slots), 1)
    return ((index == picked[:, 0:1]) | (index == picked[:, 1:2])).astype(bf16)


def experts_kernel(
    place_ref,
    places_ref,
    picked_ref,
    rows_ref,
    weight_ref,
    router_ref,
    router_wide_ref,
    slots_ref,
    named_ref,
    back_ref,
    shared_back_ref,
    dispatched_ref,
    act_ref,
    grad_pre_ref,
    grad_res_ref,
    gate_ref,
    shared_act_ref,
    shared_grad_ref,
    grad_logits_ref,
    grad_rows_ref,
    grad_gates_ref,
    grad_slots_ref,
    *,
    experts,
):
    step = pl.program_id(0)
    group = rows_ref.shape[0]
    capacity = slots_ref.shape[1]

    @pl.when(step < experts)
    def _():
        picks = slot_picks(place_ref[0], capacity)
        dispatched = dot(picks.astype(bf16), rows_ref[...]).astype(bf16)
        dispatched_ref[0] = dispatched
        pre = dot(dispatched, weight_ref[0])
        logits = dot(dispatched, router_wide_ref[...])
        lane = lax.broadcasted_iota(jnp.int32, logits.shape, 1)
        named = named_ref[0].astype(f32) > 0.0
        peak = jnp.max(jnp.where(named, logits, -jnp.inf), axis=1, keepdims=True)
        shares = jnp.where(named, jnp.exp(logits - peak), 0.0)
        total = jnp.sum(shares, axis=1, keepdims=True)
        own = jnp.sum(jnp.where(lane == step, shares, 0.0), axis=1, keepdims=True)
        gate = jnp.where(total > 0.0, own / jnp.maximum(total, 1.0), 0.0)
        gate_ref[0] = gate
        value, slope = gelu_terms(pre)
        act = value.astype(bf16)
        act_ref[0] = act
        back = back_ref[0].astype(f32)
        grad_pre = (gate * back * slope).astype(bf16)
        grad_pre_ref[0] = grad_pre
        grad_res_ref[0] = (gate * slots_ref[0].astype(f32)).astype(bf16)
        grad_gate = jnp.sum(back * act.astype(f32), axis=1, keepdims=True)
        grad_gates_ref[step] = jnp.sum(jnp.where(picks, grad_gate, 0.0), axis=0, keepdims=True)
        here = pl.ds(pl.multiple_of(step * capacity, capacity), capacity)
        grad_slots_ref[here, :] = dot(grad_pre, weight_ref[0], NT).astype(bf16)

    @pl.when(step == experts)
    def _():
        logits = dot(router_ref[...], rows_ref[...], NT)
        named = places_ref[...] >= 0
        peak = jnp.max(jnp.where(named, logits, -jnp.inf), axis=0, keepdims=True)
        shares = jnp.where(named, jnp.exp(logits - peak), 0.0)
        gates = shares / jnp.sum(shares, axis=0, keepdims=True)
        grad_gates = jnp.concatenate([grad_gates_ref[e] for e in range(experts)], axis=0)
        grad_logits = gates * (grad_gates - jnp.sum(gates * grad_gates, axis=0, keepdims=True))
        grad_logits_ref[...] = grad_logits
        high = grad_logits.astype(bf16)
        rest = (grad_logits - high.astype(f32)).astype(bf16)
        for chunk in row_chunks(group):
            value, slope = gelu_terms(dot(rows_ref[chunk, :], weight_ref[0]))
            shared_act_ref[chunk, :] = value.astype(bf16)
            grad_pre = (shared_back_ref[chunk, :].astype(f32) * slope).astype(bf16)
            shared_grad_ref[chunk, :] = grad_pre
            total = dot(slots_of(picked_ref[chunk, :], experts * capacity), grad_slots_ref[...])
            total += dot(grad_pre, weight_ref[0], NT)
            total += dot(high[:, chunk], router_ref[...], TN)
            total += dot(rest[:, chunk], router_ref[...], TN)
            grad_rows_ref[chunk, :] = total.astype(bf16)


def experts_main(places, picked, h_two, in_w, router, slots, named, back, shared_back):
    group, width = h_two.shape
    experts, capacity, hidden = back.shape
    slot_shape = jax.ShapeDtypeStruct((experts, capacity, width), bf16)
    unit_shape = jax.ShapeDtypeStruct((experts, capacity, hidden), bf16)
    return pl.pallas_call(
        functools.partial(experts_kernel, experts=experts),
        out_shape=(
            slot_shape,
            unit_shape,
            unit_shape,
            slot_shape,
            jax.ShapeDtypeStruct((experts, capacity, 1), f32),
            jax.ShapeDtypeStruct((group, hidden), bf16),
            jax.ShapeDtypeStruct((group, hidden), bf16),
            jax.ShapeDtypeStruct((experts, group), f32),
            jax.ShapeDtypeStruct((group, width), bf16),
        ),
        grid=(experts + 1,),
        in_specs=[
            per_expert(experts, 1, group),
            whole(experts, group),
            whole(group, 2),
            whole(group, width),
            per_slab(width, hidden),
            whole(experts, width),
            whole(width, LANES),
            per_expert(experts, capacity, width),
            per_expert(experts, capacity, LANES),
            per_expert(experts, capacity, hidden),
            whole(group, hidden),
        ],
        out_specs=(
            per_expert(experts, capacity, width),
            per_expert(experts, capacity, hidden),
            per_expert(experts, capacity, hidden),
            per_expert(experts, capacity, width),
            per_expert(experts, capacity, 1),
            whole(group, hidden),
            whole(group, hidden),
            whole(experts, group),
            whole(group, width),
        ),
        scratch_shapes=[
            pltpu.VMEM((experts, 1, group), f32),
            pltpu.VMEM((experts * capacity, width), bf16),
        ],
        compiler_params=pltpu.CompilerParams(vmem_limit_bytes=58 * 2**20),
        cost_estimate=pl.CostEstimate(
            flops=32 * 10**9, bytes_accessed=50 * 2**20, transcendentals=5 * 10**6
        ),
        name="experts_main",
    )(
        places.reshape(experts, 1, group),
        places,
        picked,
        h_two,
        in_w,
        router.T,
        jnp.pad(router, ((0, 0), (0, LANES - experts))),
        slots,
        named,
        back,
        shared_back,
    )


def slab_kernel(a_ref, b_ref, a_shared_ref, b_shared_ref, out_ref, *, experts):
    step = pl.program_id(0)

    @pl.when(step < experts)
    def _():
        out_ref[0] = dot(a_ref[0], b_ref[0], TN).astype(bf16)

    @pl.when(step == experts)
    def _():
        out_ref[0] = dot(a_shared_ref[...], b_shared_ref[...], TN).astype(bf16)


def slab_product(a, b, a_shared, b_shared, name):
    experts, capacity, width = a.shape
    hidden = b.shape[2]
    group = a_shared.shape[0]
    return pl.pallas_call(
        functools.partial(slab_kernel, experts=experts),
        out_shape=jax.ShapeDtypeStruct((experts + 1, width, hidden), bf16),
        grid=(experts + 1,),
        in_specs=[
            per_expert(experts, capacity, width),
            per_expert(experts, capacity, hidden),
            whole(group, width),
            whole(group, hidden),
        ],
        out_specs=per_slab(width, hidden),
        compiler_params=pltpu.CompilerParams(vmem_limit_bytes=48 * 2**20),
        cost_estimate=pl.CostEstimate(
            flops=7 * 10**9, bytes_accessed=28 * 2**20, transcendentals=0
        ),
        name=name,
    )(a, b, a_shared, b_shared)


def branch_kernel(picked_ref, gate_ref, act_ref, weight_ref, shared_ref, out_ref, res_ref, *, experts):
    step = pl.program_id(0)
    capacity = act_ref.shape[1]

    @pl.when(step < experts)
    def _():
        here = pl.ds(pl.multiple_of(step * capacity, capacity), capacity)
        res_ref[here, :] = (gate_ref[0] * dot(act_ref[0], weight_ref[0], NT)).astype(bf16)

    @pl.when(step == experts)
    def _():
        for chunk in row_chunks(out_ref.shape[0]):
            total = dot(slots_of(picked_ref[chunk, :], experts * capacity), res_ref[...])
            total += dot(shared_ref[chunk, :], weight_ref[0], NT)
            out_ref[chunk, :] = total.astype(bf16)


def experts_out(picked, gates, act, out_t, shared_act):
    experts, capacity, hidden = act.shape
    group = shared_act.shape[0]
    width = out_t.shape[1]
    return pl.pallas_call(
        functools.partial(branch_kernel, experts=experts),
        out_shape=jax.ShapeDtypeStruct((group, width), bf16),
        grid=(experts + 1,),
        in_specs=[
            whole(group, 2),
            per_expert(experts, capacity, 1),
            per_expert(experts, capacity, hidden),
            per_slab(width, hidden),
            whole(group, hidden),
        ],
        out_specs=whole(group, width),
        scratch_shapes=[pltpu.VMEM((experts * capacity, width), bf16)],
        compiler_params=pltpu.CompilerParams(vmem_limit_bytes=48 * 2**20),
        cost_estimate=pl.CostEstimate(
            flops=16 * 10**9, bytes_accessed=22 * 2**20, transcendentals=0
        ),
        name="experts_out",
    )(picked, gates, act, out_t, shared_act)


def adamw_update(master, first, second, gradient, fan_in):
    step_rate = 0.5 * fan_in ** (-0.5)
    first_new = beta_one * first + (1.0 - beta_one) * gradient
    second_new = beta_two * second + (1.0 - beta_two) * gradient * gradient
    first_hat = first_new / (1.0 - beta_one**STEP)
    second_hat = second_new / (1.0 - beta_two**STEP)
    master_new = master - step_rate * (
        first_hat / (jnp.sqrt(second_hat) + epsilon) + weight_decay * master
    )
    return (master_new, first_new, second_new, master_new.astype(bf16))


def body(
    patches,
    cotangent,
    conditioning,
    lengths,
    routes,
    ada_weight,
    ada_first,
    ada_second,
    router_weight,
    router_first,
    router_second,
    qkv_weight,
    qkv_first,
    qkv_second,
    proj_weight,
    proj_first,
    proj_second,
    shared_in_weight,
    shared_in_first,
    shared_in_second,
    shared_out_weight,
    shared_out_first,
    shared_out_second,
    expert_in_weight,
    expert_in_first,
    expert_in_second,
    expert_out_weight,
    expert_out_first,
    expert_out_second,
):
    rows, D = patches.shape
    width = lax.axis_size("mp")
    n_dp = lax.axis_size("dp")
    devices = width * n_dp
    group = rows * width
    capacity = 5 * group // 16
    heads_here = H // width
    model_rank = lax.axis_index("mp")
    item_count = lengths.shape[1]
    hidden = shared_in_weight.shape[1]
    ada_cols = ada_weight.shape[1]
    router_cols = router_weight.shape[0]

    out_slab = jnp.concatenate(
        [
            jnp.swapaxes(expert_out_weight.astype(bf16), 1, 2),
            shared_out_weight.astype(bf16).T[None],
        ],
        axis=0,
    )
    in_slab = jnp.concatenate(
        [expert_in_weight.astype(bf16), shared_in_weight.astype(bf16)[None]], axis=0
    )
    out_t = lax.all_gather(out_slab, "dp", axis=1, tiled=True)
    patches_line = Gather(after(patches, out_slab))
    proj_line = Gather(proj_weight.astype(bf16).T)
    cond_all = phase(
        [patches_line, proj_line], lax.all_gather(conditioning, "dp", axis=0, tiled=True)
    )
    cond_act = jax.nn.silu(cond_all.astype(f32)).astype(bf16)
    columns = jnp.dot(cond_act, ada_weight.astype(bf16), preferred_element_type=f32)
    columns = jnp.repeat(columns.reshape(n_dp, item_count * ada_cols), width, axis=0)
    router_low = router_weight.astype(bf16).astype(f32)
    payload = jnp.concatenate(
        [columns, jnp.broadcast_to(router_low[None], (devices, router_cols))], axis=1
    )
    received = phase(
        [patches_line, proj_line], lax.all_to_all(payload, ("dp", "mp"), 0, 0, tiled=True)
    )
    qkv_here = lax.all_gather(
        after(qkv_weight.astype(bf16), received), "dp", axis=0, tiled=True
    )
    modulation = (
        received[:, : item_count * ada_cols]
        .reshape(devices, item_count, ada_cols)
        .transpose(1, 0, 2)
        .reshape(item_count, devices * ada_cols)
    )
    router_matrix = received[:, item_count * ada_cols :].reshape(D, E).astype(bf16)
    qkv_wide = jnp.pad(qkv_here.reshape(D, heads_here * 3, HD), ((0, 0), (0, 0), (0, LANES - HD)))
    qkv_wide = qkv_wide.reshape(D, heads_here * 3 * LANES)

    bounds = jnp.cumsum(lengths[0])
    places = jnp.arange(group, dtype=jnp.int32)
    segment = jnp.sum((places[:, None] >= bounds[None, :]).astype(jnp.int32), axis=1)
    segment_column = segment[:, None]
    segment_mine = lax.dynamic_slice_in_dim(segment_column, model_rank * rows, rows, 0)
    start, kind = key_windows(lengths[0], group)

    chosen = routes[:, :, None] == jnp.arange(E, dtype=jnp.int32)[None, None, :]
    names = chosen.any(axis=1)
    below = (places[:, None] > places[None, :]).astype(bf16)
    earlier = jnp.dot(below, names.astype(bf16), preferred_element_type=f32).astype(jnp.int32)
    place_of = jnp.where(names, earlier, -1).T
    picked = routes * capacity + jnp.sum(jnp.where(chosen, earlier[:, None, :], 0), axis=2)
    names_low = jnp.pad(names.astype(bf16), ((0, 0), (0, LANES - E)))
    lane = jnp.arange(qkv_wide.shape[1], dtype=jnp.int32)
    item, role = lane % LANES - HD, lane // LANES % 3
    same = segment[:, None] == item[None, :]
    marks = jnp.where(
        same, jnp.where(role == 0, FAR, 0.0)[None, :], jnp.where(role == 1, -FAR, 0.0)[None, :]
    )
    marks = jnp.where(((item >= 0) & (item < item_count))[None, :], marks, 0.0)
    modulation, router_matrix, qkv_wide, place_of, picked = phase(
        [patches_line, proj_line], (modulation, router_matrix, qkv_wide, place_of, picked)
    )

    cot_line = Gather(after(cotangent, patches_line.ups[-1]))
    patches_all, h_one_all = norm_one(patches_line.blocks(), modulation, segment_column)
    proj_rows = proj_line.whole(axis=1)
    qkv = (jnp.dot(h_one_all, qkv_wide, preferred_element_type=f32) + marks).astype(bf16)
    qkv, proj_rows = phase([cot_line], (qkv, proj_rows))
    (mixed_here, logs), out_t = phase([cot_line], (attend(qkv, start, kind), out_t))
    in_w = lax.all_gather(after(in_slab, out_t), "dp", axis=1, tiled=True)
    mixed_line = Gather(mixed_here)
    half = proj_rows.shape[1] // 2
    proj_first_half = phase(
        [cot_line, mixed_line], lax.all_gather(proj_rows[:, :half], "dp", axis=0, tiled=True)
    )
    gate_two = modulation[:, 5 * D :]
    gate_rows = functools.reduce(
        lambda kept, i: jnp.where(segment_column >= i, gate_two[i : i + 1], kept),
        range(1, item_count),
        gate_two[0:1],
    )
    grad_branch = (gate_rows * cot_line.whole().astype(f32)).astype(bf16)
    branch_slots, named_slots, back_slots, back_shared = phase(
        [mixed_line], experts_before(place_of, names_low, grad_branch, out_t, capacity)
    )
    proj_other_half = phase(
        [mixed_line], lax.all_gather(proj_rows[:, half:], "dp", axis=0, tiled=True)
    )
    proj = jnp.concatenate([proj_first_half, proj_other_half], axis=1).T
    h_two, x_one_mine, attn_mine, mixed_mine = norm_two(
        mixed_line.blocks(), patches_all, proj, modulation, segment_column
    )

    (
        dispatched,
        expert_act,
        grad_expert_pre,
        grad_res,
        gates,
        shared_act,
        grad_shared_pre,
        grad_logits,
        grad_h_two,
    ) = experts_main(
        place_of,
        picked,
        h_two,
        in_w,
        router_matrix,
        branch_slots,
        named_slots,
        back_slots,
        back_shared,
    )
    two_line = Scatter(grad_h_two)
    grad_out_slab = phase(
        [two_line], slab_product(grad_res, expert_act, grad_branch, shared_act, "grad_out")
    )
    grad_out_mine = lax.psum_scatter(grad_out_slab, "dp", scatter_dimension=1, tiled=True)
    grad_in_slab = phase(
        [two_line], slab_product(dispatched, grad_expert_pre, h_two, grad_shared_pre, "grad_in")
    )
    grad_router = phase(
        [two_line],
        jnp.einsum("gd,eg->de", h_two.astype(f32), grad_logits, precision=highest),
    )
    grad_x_one, grad_attn, grad_mixed_mine, sums_two = back_two(
        two_line.terms(), x_one_mine, attn_mine, cotangent, proj, modulation, segment_mine
    )
    grad_mixed, mlp_part = phase(
        [],
        (
            lax.all_to_all(
                grad_mixed_mine.reshape(width, heads_here * HD, rows), "mp", 0, 0, tiled=True
            ),
            experts_out(
                picked, after(gates, grad_mixed_mine), expert_act, out_t, shared_act
            ),
        ),
    )
    grad_mixed = grad_mixed.transpose(1, 0, 2).reshape(heads_here * HD, group)
    mlp_line = Scatter(mlp_part)
    grad_proj_t = jnp.einsum("gd,cg->dc", grad_attn, mixed_mine, preferred_element_type=f32)
    proj_sums = Scatter(grad_proj_t.astype(bf16), axis=1)
    grad_qkv, grad_out_mine = phase(
        [mlp_line, proj_sums], (attend_back(qkv, grad_mixed, logs, start, kind), grad_out_mine)
    )
    grad_in_mine = lax.psum_scatter(
        after(grad_in_slab, grad_out_mine), "dp", scatter_dimension=1, tiled=True
    )
    partial = phase(
        [mlp_line, proj_sums],
        jnp.einsum("gc,dc->gd", grad_qkv, qkv_wide, preferred_element_type=f32).astype(bf16),
    )
    one_line = Scatter(partial)
    grad_qkv_weight = jnp.einsum("gd,gc->dc", h_one_all, grad_qkv, preferred_element_type=f32)
    grad_qkv_weight = grad_qkv_weight.reshape(D, heads_here * 3, LANES)[:, :, :HD]
    grad_qkv_weight = phase(
        [one_line, mlp_line, proj_sums], grad_qkv_weight.reshape(D, heads_here * 3 * HD).astype(bf16)
    )
    result, sums_gate = phase(
        [one_line], outcome(mlp_line.terms(), x_one_mine, cotangent, modulation, segment_mine)
    )
    grad_attn_slab, grad_in_mine = phase(
        [one_line],
        (
            jnp.concatenate([grad_qkv_weight, proj_sums.total().astype(bf16)], axis=1),
            grad_in_mine,
        ),
    )
    grad_attn_mine = lax.psum_scatter(
        after(grad_attn_slab, grad_in_mine), "dp", scatter_dimension=0, tiled=True
    ).astype(f32)
    patch_grad, sums_one = back_one(
        one_line.terms(), patches, grad_x_one, modulation, segment_mine
    )
    grad_modulation = jnp.concatenate([sums_one, sums_two, sums_gate], axis=1)
    payload = jnp.concatenate(
        [
            grad_modulation.reshape(item_count, devices, ada_cols)
            .transpose(1, 0, 2)
            .reshape(devices, item_count * ada_cols),
            grad_router.reshape(devices, router_cols),
        ],
        axis=1,
    )
    received = lax.all_to_all(payload, ("dp", "mp"), 0, 0, tiled=True)
    router_grad = jnp.sum(received[:, item_count * ada_cols :], axis=0)
    columns = jnp.sum(
        received[:, : item_count * ada_cols].reshape(n_dp, width, item_count, ada_cols), axis=1
    ).reshape(n_dp * item_count, ada_cols)
    ada_grad = jnp.einsum("id,ic->dc", cond_act.astype(f32), columns, precision=highest)
    grad_out_mine, grad_in_mine = grad_out_mine.astype(f32), grad_in_mine.astype(f32)

    qkv_cols = qkv_weight.shape[1]
    gradients = (
        ada_grad,
        router_grad,
        grad_attn_mine[:, :qkv_cols],
        grad_attn_mine[:, qkv_cols:].T,
        grad_in_mine[E],
        grad_out_mine[E].T,
        grad_in_mine[:E],
        jnp.swapaxes(grad_out_mine[:E], 1, 2),
    )
    states_of = (
        (ada_weight, ada_first, ada_second),
        (router_weight, router_first, router_second),
        (qkv_weight, qkv_first, qkv_second),
        (proj_weight, proj_first, proj_second),
        (shared_in_weight, shared_in_first, shared_in_second),
        (shared_out_weight, shared_out_first, shared_out_second),
        (expert_in_weight, expert_in_first, expert_in_second),
        (expert_out_weight, expert_out_first, expert_out_second),
    )
    total_hidden = float(hidden * width)
    fan_ins = (D, D, D, 8.0 * D / group, D, total_hidden, D, total_hidden)
    updates = []
    for (master, first, second), gradient, fan_in in zip(states_of, gradients, fan_ins):
        updates.extend(adamw_update(master, first, second, gradient, float(fan_in)))
    return tuple([result, patch_grad] + updates)


def solution(mesh):
    tokens, data = P(("dp", "mp"), None), P("dp", None)
    ada, router = P(None, ("dp", "mp")), P(("dp", "mp"))
    deep, wide = P("dp", "mp"), P("mp", "dp")
    deep_experts, wide_experts = P(None, "dp", "mp"), P(None, "mp", "dp")
    kinds = (ada, router, deep, wide, deep, wide, deep_experts, wide_experts)
    in_specs = (tokens, tokens, data, data, data) + tuple(k for k in kinds for _ in range(3))
    out_specs = (tokens, tokens) + tuple(k for k in kinds for _ in range(4))
    return jax.shard_map(body, mesh=mesh, in_specs=in_specs, out_specs=out_specs, check_vma=False)
```

time: 888 us -> 639 us (0.72)
  matrix products: 269 us -> 16 us
  Pallas kernels: 0 us -> 206 us
  waiting for transfers between devices: 180 us -> 82.2 us
  other arithmetic: 157 us -> 68.9 us
  blocking collectives: 24 us -> 47.8 us
  local copies, waits for them, and re-layouts: 83 us -> 64.4 us
  loops' own time: 12 us -> 0 us
    dot_general x43 -> x3, matrix products: 258 us -> 7.75 us  [the longest x1 3.56 us: body(): jnp.dot(h_one_all, qkv_wide, preferred_element_type=f32) + marks]
    pallas_call x0 -> x12, Pallas kernels: none -> 206 us  [the longest x1 74.1 us: experts_main(): pl.pallas_call(functools.partial(experts_kernel, experts=experts), out_sh...]
    reduce_scatter x1, waiting for transfers between devices: 65.3 us -> 0.01 us  [body(): lax.psum_scatter(after(grad_in_slab, grad_out_mine), 'dp', scatter_dimens...]
    ppermute x48, waiting for transfers between devices: 109 us -> 59.4 us  [the longest x12 34.1 us: send(): lax.ppermute(up, 'mp', [(i, i + 1) for i in range(step)])]
    convert_element_type x23 -> x14, other arithmetic: 74.3 us -> 26.7 us  [the longest x8 14.4 us: send(): down = (down.astype(f32) + self.down.astype(f32)).astype(bf16)]
    all_gather x2 -> x4, blocking collectives: 24 us -> 47.8 us  [the longest x1 16.1 us: body(): lax.all_gather(proj_rows[:, :half], 'dp', axis=0, tiled=True)]
    reduce_sum x15 -> x2, other arithmetic: 19.8 us -> 0.13 us  [the longest x1 0.09 us: key_windows(): jnp.sum((high - low)[:, None] > widths[None, :], axis=1).astype(jnp.int32)]
    dynamic_update_slice x12 -> x0, other arithmetic: 15.6 us -> none  [the longest x9 13.8 us: line_gather(): whole = lax.dynamic_update_slice_in_dim(whole, piece, owner * rows, 0)]
  transfers between devices with their start and end apart: 57 -> 56, of which waited for: 22 -> 13; matrix products, arithmetic and copies ran while one was open for 45% -> 18% of each run, Pallas kernels for 0% -> 21%
where the time goes in v2:
time: 639 us; the launch traced here: 632 us
  Pallas kernels  206 us (32%)
  starting transfers between devices  130 us (20%)
  waiting for transfers between devices  82.2 us (13%)
  other arithmetic  68.9 us (11%)
  local copies, waits for them, and re-layouts  64.4 us (10%)
  blocking collectives  47.8 us (7%)
  between operations  16.1 us (3%)
  matrix products  16 us (3%)
    pallas_call x1, Pallas kernels, experts_main(): pl.pallas_call(functools.partial(experts_kernel, experts=experts), out_sh...  74.1 us
    ppermute x12, starting transfers between devices, send(): lax.ppermute(up, 'mp', [(i, i + 1) for i in range(step)])  50.5 us
    ppermute x12, waiting for transfers between devices, send(): lax.ppermute(up, 'mp', [(i, i + 1) for i in range(step)])  34.1 us
    ppermute x12, starting transfers between devices, send(): lax.ppermute(self.ups[-1], 'mp', up_pairs)  33.2 us
    unnamed x202, local copies, waits for them, and re-layouts  32 us
    pallas_call x2, Pallas kernels, slab_product(): pl.pallas_call(functools.partial(slab_kernel, experts=experts), out_shape...  29.9 us
    pallas_call x1, Pallas kernels, experts_out(): pl.pallas_call(functools.partial(branch_kernel, experts=experts), out_sha...  24.4 us
    pallas_call x1, Pallas kernels, experts_before(): pl.pallas_call(functools.partial(before_kernel, experts=experts), out_sha...  23.1 us
  transfers between devices with their start and end apart: 56, of which 13 were waited for; matrix products, arithmetic and copies ran while one was open for 18% of the time, Pallas kernels for 21%

profile of v2, /device:TPU:0, one launch (start us, length us, event | category | flops | bytes accessed | tf_op | source)
XLA Modules:
  0.0 632.1 jit_solution(8861895593329099654)
XLA Ops:
  10.4 5.9 collective-permute-start
  18.4 5.2 collective-permute-start.2
  28.9 9.2 %all-gather = bf16[8,3,768]{2,1,0:T(4,128)(2,1)S(1)} all-gather(bf16[1,3,768]{2,1,0:T(4,128)(2,1)S(1)} %bitcast.113), channel_id=1, replica_groups=mesh['dp'=8,'mp'=4] {'dp'}, dimensions={0}, use_global_device_ids=true | all-gather | bytes 41472 | tf_op jit(solution)/shard_map/all_gather | solution.py:886
  42.1 8.6 %all-to-all-start = ((f32[32,1,624]{2,1,0:T(1,128)}), f32[32,1,624]{2,1,0:T(1,128)S(1)}, u32[]{:S(2)}, u32[]{:S(2)}) async-start(f32[32,1,624]{2,1,0:T(1,128)} %all_to_all.19), calls=%async_computation | async-start | bytes 163840 | tf_op jit(solution)/shard_map/all_to_all | solution.py:896
  53.4 10.6 %all-to-all-done = f32[32,1,624]{2,1,0:T(1,128)S(1)} async-done(((f32[32,1,624]{2,1,0:T(1,128)}), f32[32,1,624]{2,1,0:T(1,128)S(1)}, u32[]{:S(2)}, u32[]{:S(2)}) %all-to-all-start) | async-done | bytes 79904 | tf_op jit(solution)/shard_map/all_to_all | solution.py:896
  75.4 11.7 %all_gather.19 = bf16[768,576]{1,0:T(8,128)(2,1)} all-gather(bf16[96,576]{1,0:T(8,128)(2,1)S(1)} %convert_element_type.277), channel_id=1, replica_groups=mesh['dp'=8,'mp'=4] {'dp'}, dimensions={0}, use_global_device_ids=true | all-gather | bytes 995328 | tf_op jit(solution)/shard_map/all_gather | solution.py:898
  94.7 6.0 collective-permute-start.12
  120.1 14.5 %attend.1 = (bf16[192,1536]{1,0:T(8,128)(2,1)S(1)}, f32[3,1,1536]{2,1,0:T(1,128)S(1)}) custom-call(s32[6]{0:T(128)S(1)} %subtract_minimum_fusion.start_ref, s32[6]{0:T(128)S(1)} %convert_reduce_fusion.1.kind_ref, bf16[1536,1152]{1,0:T(8,128)(2,1)S(1)} %fusion.1.qkv_ref), custom_call_target="tpu_custom_call" | custom-call | flops 7247757312 | bytes 6291456 | tf_op jit(solution)/shard_map/attend/pallas_call | solution.py:174
  136.1 5.4 collective-permute-start.18
  147.2 16.1 %all_gather.21 = bf16[768,384]{1,0:T(8,128)(2,1)} all-gather(bf16[96,384]{1,0:T(8,128)(2,1)S(1)} %get-tuple-element.503), channel_id=1, replica_groups=mesh['dp'=8,'mp'=4] {'dp'}, dimensions={0}, use_global_device_ids=true | all-gather | bytes 663552 | tf_op jit(solution)/shard_map/all_gather | solution.py:946
  163.3 7.9 %collective-permute-done.17 = bf16[384,768]{1,0:T(8,128)(2,1)} collective-permute-done((bf16[384,768]{1,0:T(8,128)(2,1)}, bf16[384,768]{1,0:T(8,128)(2,1)}, u32[]{:S(2)}, u32[]{:S(2)}) %collective-permute-start.17) | collective-permute-done | bytes 589856 | tf_op jit(solution)/shard_map/ppermute | solution.py:52
  176.0 6.1 multiply_convert_fusion.branch_ref.a_shared_ref
  182.1 23.1 %experts_before.1 = (bf16[8,480,768]{2,1,0:T(8,128)(2,1)}, bf16[8,480,128]{2,1,0:T(8,128)(2,1)S(1)}, bf16[8,480,768]{2,1,0:T(8,128)(2,1)}, bf16[1536,768]{1,0:T(8,128)(2,1)S(1)}) custom-call(s32[8,1,1536]{2,1,0:T(1,128)S(1)} %copy.182.place_ref, bf16[1536,128]{1,0:T(8,128)(2,1)S(1)} %pad_convert_fusion.named_ref, ...), custom_call_target="tpu_custom_call" | custom-call | flops 16000000000 | bytes 31457280 | tf_op jit(solution)/shard_map/experts_before/pallas_call | solution.py:557
  210.4 10.8 %all_gather.22 = bf16[768,384]{1,0:T(8,128)(2,1)} all-gather(bf16[96,384]{1,0:T(8,128)(2,1)S(1)} %get-tuple-element.502), channel_id=1, replica_groups=mesh['dp'=8,'mp'=4] {'dp'}, dimensions={0}, use_global_device_ids=true | all-gather | bytes 663552 | tf_op jit(solution)/shard_map/all_gather | solution.py:959
  233.9 9.7 %norm_two.1 = (bf16[1536,768]{1,0:T(8,128)(2,1)S(1)}, f32[384,768]{1,0:T(8,128)S(1)}, f32[384,768]{1,0:T(8,128)S(1)}, bf16[768,384]{1,0:T(8,128)(2,1)S(1)}) custom-call(s32[1]{0:T(128)} %bitcast.12.refs_0_, s32[1536,1]{1,0:T(8,128)S(1)} %copy-done.9, f32[3,4608]{1,0:T(4,128)S(1)} %copy-done.17, bf16[1536,768]{1,0:T(8,128)(2,1)S(1)} %copy-done.32, ...), custom_call_target="tpu_custom_call" | custom-call | flops 2000000000 | bytes 13631488 | tf_op jit(solution)/shard_map/norm_two/pallas_call | solution.py:358
  247.9 74.1 %experts_main.1 = (bf16[8,480,768]{2,1,0:T(8,128)(2,1)}, bf16[8,480,768]{2,1,0:T(8,128)(2,1)}, bf16[8,480,768]{2,1,0:T(8,128)(2,1)}, bf16[8,480,768]{2,1,0:T(8,1...) custom-call(s32[8,1,1536]{2,1,0:T(1,128)} %copy-done.28, ...), custom_call_target="tpu_custom_call" | custom-call | flops 32000000000 | bytes 52428800 | tf_op jit(solution)/shard_map/experts_main/pallas_call | solution.py:677
  330.0 14.3 %grad_out.1 = bf16[9,768,768]{2,1,0:T(8,128)(2,1)} custom-call(bf16[8,480,768]{2,1,0:T(8,128)(2,1)} %get-tuple-element.204.a_ref, bf16[8,480,768]{2,1,0:T(8,128)(2,1)} %get-tuple-element.205.b_ref.act_ref, bf16[1536,768]{1,0:T(8,128)(2,1)S(1)} %multiply_convert_fusion.branch_ref.a_shared_ref, bf16[1536,768]{1,0:T(8,128)(2,1)S(1)} %copy-done.10), custom_call_target="tpu_custom_call" | custom-call | flops 7000000000 | bytes 29360128 | tf_op jit(solution)/shard_map/grad_out/pallas_call | solution.py:755
  353.2 15.6 %grad_in.1 = bf16[9,768,768]{2,1,0:T(8,128)(2,1)} custom-call(bf16[8,480,768]{2,1,0:T(8,128)(2,1)} %get-tuple-element.209.a_ref, bf16[8,480,768]{2,1,0:T(8,128)(2,1)} %get-tuple-element.210.b_ref, bf16[1536,768]{1,0:T(8,128)(2,1)S(1)} %copy-done.1, bf16[1536,768]{1,0:T(8,128)(2,1)S(1)} %copy-done.11), custom_call_target="tpu_custom_call" | custom-call | flops 7000000000 | bytes 29360128 | tf_op jit(solution)/shard_map/grad_in/pallas_call | solution.py:755
  379.0 8.9 %collective-permute-done.28.up_ref = bf16[384,768]{1,0:T(8,128)(2,1)} collective-permute-done((bf16[384,768]{1,0:T(8,128)(2,1)}, bf16[384,768]{1,0:T(8,128)(2,1)}, u32[]{:S(2)}, u32[]{:S(2)}) %collective-permute-start.28) | collective-permute-done | bytes 589856 | tf_op jit(solution)/shard_map/ppermute | solution.py:100
  387.9 5.0 collective-permute-done.29.down_ref
  395.2 4.9 back_two.1
  414.2 24.4 %experts_out.1 = bf16[1536,768]{1,0:T(8,128)(2,1)S(1)} custom-call(s32[1536,2]{1,0:T(8,128)S(1)} %copy-done.22, f32[8,480,1]{2,1,0:T(8,128)S(1)} %copy-done.39, bf16[8,480,768]{2,1,0:T(8,128)(2,1)} %get-tuple-element.205.b_ref.act_ref, bf16[9,768,768]{2,1,0:T(8,128)(2,1)} %all-gather.4.cloned.1.call-done.weight_ref, ...), custom_call_target="tpu_custom_call" | custom-call | flops 16000000000 | bytes 23068672 | tf_op jit(solution)/shard_map/experts_out/pallas_call | solution.py:795
  444.4 18.4 %attend_back.1 = bf16[1536,1152]{1,0:T(8,128)(2,1)S(1)} custom-call(s32[6]{0:T(128)S(1)} %subtract_minimum_fusion.start_ref, s32[6]{0:T(128)S(1)} %convert_reduce_fusion.1.kind_ref, bf16[1536,1152]{1,0:T(8,128)(2,1)S(1)} %copy-done.38, bf16[192,1536]{1,0:T(8,128)(2,1)S(1)} %bitcast.99, f32[3,1,1536]{2,1,0:T(1,128)S(1)} %get-tuple-element.226.log_ref), custom_call_target="tpu_custom_call" | custom-call | flops 18119393280 | bytes 12582912 | tf_op jit(solution)/shard_map/attend_back/pallas_call | solution.py:238
  484.3 9.8 %collective-permute-done.34 = bf16[384,768]{1,0:T(8,128)(2,1)S(1)} collective-permute-done((bf16[384,768]{1,0:T(8,128)(2,1)S(1)}, bf16[384,768]{1,0:T(8,128)(2,1)S(1)}, u32[]{:S(2)}, u32[]{:S(2)}) %collective-permute-start.34) | collective-permute-done | bytes 589856 | tf_op jit(solution)/shard_map/ppermute | solution.py:100
  495.0 7.6 %collective-permute-start.42 = (bf16[768,192]{0,1:T(8,128)(2,1)S(1)}, bf16[768,192]{0,1:T(8,128)(2,1)S(1)}, u32[]{:S(2)}, u32[]{:S(2)}) collective-permute-start(bf16[768,192]{0,1:T(8,128)(2,1)S(1)} %get-tuple-element.497), channel_id=1, source_target_pairs={{0,1},{1,2},{2,3},{4,5},{5,6},{6,7},{8,9},{9,10},{10,11},{12,13},{... | collective-permute-start | bytes 884744 | tf_op jit(solution)/shard_map/ppermute | solution.py:100
  512.2 5.4 collective-permute-start.38
  531.4 5.1 collective-permute-done.38
  544.0 6.9 %fusion.34 = (bf16[8,768,96]{1,2,0:T(8,128)(2,1)}, f32[8,768,96]{1,2,0:T(8,128)}, f32[8,768,96]{1,2,0:T(8,128)}, f32[8,768,96]{1,2,0:T(8,128)}) fusion(f32[8,768,96]{1,2,0:T(8,128)S(1)} %copy-done.44, f32[9,96,768]{2,1,0:T(8,128)S(1)} %copy-done.43, f32[8,768,96]{1,2,0:T(8,128)} %param.57, f32[8,768,96]{1,2,0:T(8,128)} %param.58), kind=kLoop, calls=%fused_computation.163 | loop fusion | flops 9437184 | bytes 17694720 | tf_op jit(solution)/shard_map/convert_element_type | solution.py:825
  556.1 8.3 %collective-permute-start.46 = (bf16[384,768]{1,0:T(8,128)(2,1)S(1)}, bf16[384,768]{1,0:T(8,128)(2,1)S(1)}, u32[]{:S(2)}, u32[]{:S(2)}) collective-permute-start(bf16[384,768]{1,0:T(8,128)(2,1)S(1)} %get-tuple-element.472), channel_id=1, source_target_pairs={{0,1},{1,2},{2,3},{4,5},{5,6},{6,7},{8,9},{9,10},{10,11},{12,13},{... | collective-permute-start | bytes 1769480 | tf_op jit(solution)/shard_map/ppermute | solution.py:100
  569.1 6.9 %collective-permute-done.46.up_ref = bf16[384,768]{1,0:T(8,128)(2,1)S(1)} collective-permute-done((bf16[384,768]{1,0:T(8,128)(2,1)S(1)}, bf16[384,768]{1,0:T(8,128)(2,1)S(1)}, u32[]{:S(2)}, u32[]{:S(2)}) %collective-permute-start.46) | collective-permute-done | bytes 589856 | tf_op jit(solution)/shard_map/ppermute | solution.py:100
  593.9 8.4 %fusion.36 = (bf16[8,96,768]{2,1,0:T(8,128)(2,1)}, f32[8,96,768]{2,1,0:T(8,128)}, f32[8,96,768]{2,1,0:T(8,128)}, f32[8,96,768]{2,1,0:T(8,128)}) fusion(f32[8,96,768]{2,1,0:T(8,128)} %param.53, f32[9,96,768]{2,1,0:T(8,128)} %convert_element_type.345, f32[8,96,768]{2,1,0:T(8,128)} %param.54, f32[8,96,768]{2,1,0:T(8,128)} %param.55), kind=kLoop, calls=%fused_computation.164 | loop fusion | flops 9437184 | bytes 17694720 | tf_op jit(solution)/shard_map/convert_element_type | solution.py:825
  607.4 12.2 %reduce-scatter.10.cloned.1.call-done = bf16[96,768]{1,0:T(8,128)(2,1)} async-done(((bf16[768,768]{1,0:T(8,128)(2,1)}), bf16[96,768]{1,0:T(8,128)(2,1)}) %reduce-scatter.10.cloned.1.call-update) | async-done | bytes 147472
  (419 shorter events, 228.9 us)
Async XLA Ops:
  7.2 128.3 %all-gather.4.cloned.1.call-start = ((), (), s32[]{:S(2)}) async-start(), calls=%async_computation.6 | async-start | bytes 11943936 | tf_op jit(solution)/shard_map/all_gather | solution.py:882
  10.4 27.8 %collective-permute-start = (bf16[384,768]{1,0:T(8,128)(2,1)S(1)}, bf16[384,768]{1,0:T(8,128)(2,1)}, u32[]{:S(2)}, u32[]{:S(2)}) collective-permute-start(bf16[384,768]{1,0:T(8,128)(2,1)S(1)} %copy-done.13), channel_id=1, source_target_pairs={{0,1},{1,2},{2,3},{4,5},{5,6},{6,7},{8,9},{9,10},{10,11},{12,13},{... | collective-permute-start | bytes 1769480 | tf_op jit(solution)/shard_map/ppermute | solution.py:51
  16.3 21.9 %collective-permute-start.1 = (bf16[384,768]{1,0:T(8,128)(2,1)S(1)}, bf16[384,768]{1,0:T(8,128)(2,1)}, u32[]{:S(2)}, u32[]{:S(2)}) collective-permute-start(bf16[384,768]{1,0:T(8,128)(2,1)S(1)} %copy-done.13), channel_id=1, source_target_pairs={{1,0},{2,1},{3,2},{5,4},{6,5},{7,6},{9,8},{10,9},{11,10},{13,12},{... | collective-permute-start | bytes 1769480 | tf_op jit(solution)/shard_map/ppermute | solution.py:52
  38.2 25.8 %collective-permute-start.4 = (bf16[384,768]{1,0:T(8,128)(2,1)}, bf16[384,768]{1,0:T(8,128)(2,1)}, u32[]{:S(2)}, u32[]{:S(2)}) collective-permute-start(bf16[384,768]{1,0:T(8,128)(2,1)} %collective-permute-done), channel_id=1, source_target_pairs={{1,2},{2,3},{5,6},{6,7},{9,10},{10,11},{13,14},{14,15},{17,18},{18... | collective-permute-start | bytes 1769480 | tf_op jit(solution)/shard_map/ppermute | solution.py:51
  39.7 24.3 %collective-permute-start.5 = (bf16[384,768]{1,0:T(8,128)(2,1)}, bf16[384,768]{1,0:T(8,128)(2,1)}, u32[]{:S(2)}, u32[]{:S(2)}) collective-permute-start(bf16[384,768]{1,0:T(8,128)(2,1)} %collective-permute-done.1), channel_id=1, source_target_pairs={{1,0},{2,1},{5,4},{6,5},{9,8},{10,9},{13,12},{14,13},{17,16},{18,1... | collective-permute-start | bytes 1769480 | tf_op jit(solution)/shard_map/ppermute | solution.py:52
  42.1 22.0 %all-to-all-start = ((f32[32,1,624]{2,1,0:T(1,128)}), f32[32,1,624]{2,1,0:T(1,128)S(1)}, u32[]{:S(2)}, u32[]{:S(2)}) async-start(f32[32,1,624]{2,1,0:T(1,128)} %all_to_all.19), calls=%async_computation | async-start | bytes 163840 | tf_op jit(solution)/shard_map/all_to_all | solution.py:896
  50.7 197.2 %all-gather.6.cloned.1.call-start = ((), (), s32[]{:S(2)}) async-start(), calls=%async_computation.7 | async-start | bytes 11943936 | tf_op jit(solution)/shard_map/all_gather | solution.py:942
  64.1 30.6 %collective-permute-start.8 = (bf16[384,768]{1,0:T(8,128)(2,1)}, bf16[384,768]{1,0:T(8,128)(2,1)}, u32[]{:S(2)}, u32[]{:S(2)}) collective-permute-start(bf16[384,768]{1,0:T(8,128)(2,1)} %collective-permute-done.4), channel_id=1, source_target_pairs={{2,3},{6,7},{10,11},{14,15},{18,19},{22,23},{26,27},{30,31}} | collective-permute-start | bytes 1769480 | tf_op jit(solution)/shard_map/ppermute | solution.py:51
  65.6 29.1 %collective-permute-start.9 = (bf16[384,768]{1,0:T(8,128)(2,1)}, bf16[384,768]{1,0:T(8,128)(2,1)}, u32[]{:S(2)}, u32[]{:S(2)}) collective-permute-start(bf16[384,768]{1,0:T(8,128)(2,1)} %collective-permute-done.5), channel_id=1, source_target_pairs={{1,0},{5,4},{9,8},{13,12},{17,16},{21,20},{25,24},{29,28}} | collective-permute-start | bytes 1769480 | tf_op jit(solution)/shard_map/ppermute | solution.py:52
  71.7 22.9 %collective-permute-start.10 = (bf16[96,192]{1,0:T(8,128)(2,1)}, bf16[96,192]{1,0:T(8,128)(2,1)}, u32[]{:S(2)}, u32[]{:S(2)}) collective-permute-start(bf16[96,192]{1,0:T(8,128)(2,1)} %collective-permute-done.6), channel_id=1, source_target_pairs={{2,3},{6,7},{10,11},{14,15},{18,19},{22,23},{26,27},{30,31}} | collective-permute-start | bytes 110600 | tf_op jit(solution)/shard_map/ppermute | solution.py:51
  73.0 21.6 %collective-permute-start.11 = (bf16[96,192]{1,0:T(8,128)(2,1)}, bf16[96,192]{1,0:T(8,128)(2,1)}, u32[]{:S(2)}, u32[]{:S(2)}) collective-permute-start(bf16[96,192]{1,0:T(8,128)(2,1)} %collective-permute-done.7), channel_id=1, source_target_pairs={{1,0},{5,4},{9,8},{13,12},{17,16},{21,20},{25,24},{29,28}} | collective-permute-start | bytes 110600 | tf_op jit(solution)/shard_map/ppermute | solution.py:52
  135.6 329.1 %reduce-scatter.6.cloned.1.call-start = ((), (), s32[]{:S(2)}) async-start(), calls=%async_computation.8 | async-start | bytes 11943936 | tf_op jit(solution)/shard_map/reduce_scatter | solution.py:991
  136.1 35.1 %collective-permute-start.18 = (bf16[192,1536]{1,0:T(8,128)(2,1)S(1)}, bf16[192,1536]{1,0:T(8,128)(2,1)}, u32[]{:S(2)}, u32[]{:S(2)}) collective-permute-start(bf16[192,1536]{1,0:T(8,128)(2,1)S(1)} %get-tuple-element.179.refs_5_), channel_id=1, source_target_pairs={{0,1},{1,2},{2,3},{4,5},{5,6},{6,7},{8,9},{9,10},{10,11},{12,13},{... | collective-permute-start | bytes 1769480 | tf_op jit(solution)/shard_map/ppermute | solution.py:51
  141.5 29.7 %collective-permute-start.19 = (bf16[192,1536]{1,0:T(8,128)(2,1)S(1)}, bf16[192,1536]{1,0:T(8,128)(2,1)}, u32[]{:S(2)}, u32[]{:S(2)}) collective-permute-start(bf16[192,1536]{1,0:T(8,128)(2,1)S(1)} %get-tuple-element.179.refs_5_), channel_id=1, source_target_pairs={{1,0},{2,1},{3,2},{5,4},{6,5},{7,6},{9,8},{10,9},{11,10},{13,12},{... | collective-permute-start | bytes 1769480 | tf_op jit(solution)/shard_map/ppermute | solution.py:52
  142.8 20.5 %collective-permute-start.16 = (bf16[384,768]{1,0:T(8,128)(2,1)}, bf16[384,768]{1,0:T(8,128)(2,1)}, u32[]{:S(2)}, u32[]{:S(2)}) collective-permute-start(bf16[384,768]{1,0:T(8,128)(2,1)} %copy-done.66), channel_id=1, source_target_pairs={{2,3},{6,7},{10,11},{14,15},{18,19},{22,23},{26,27},{30,31}} | collective-permute-start | bytes 1769480 | tf_op jit(solution)/shard_map/ppermute | solution.py:51
  144.3 26.9 %collective-permute-start.17 = (bf16[384,768]{1,0:T(8,128)(2,1)}, bf16[384,768]{1,0:T(8,128)(2,1)}, u32[]{:S(2)}, u32[]{:S(2)}) collective-permute-start(bf16[384,768]{1,0:T(8,128)(2,1)} %collective-permute-done.15), channel_id=1, source_target_pairs={{1,0},{5,4},{9,8},{13,12},{17,16},{21,20},{25,24},{29,28}} | collective-permute-start | bytes 1769480 | tf_op jit(solution)/shard_map/ppermute | solution.py:52
  171.2 36.4 %collective-permute-start.20 = (bf16[192,1536]{1,0:T(8,128)(2,1)}, bf16[192,1536]{1,0:T(8,128)(2,1)}, u32[]{:S(2)}, u32[]{:S(2)}) collective-permute-start(bf16[192,1536]{1,0:T(8,128)(2,1)} %collective-permute-done.18), channel_id=1, source_target_pairs={{1,2},{2,3},{5,6},{6,7},{9,10},{10,11},{13,14},{14,15},{17,18},{18... | collective-permute-start | bytes 1769480 | tf_op jit(solution)/shard_map/ppermute | solution.py:51
  172.7 34.9 %collective-permute-start.21 = (bf16[192,1536]{1,0:T(8,128)(2,1)}, bf16[192,1536]{1,0:T(8,128)(2,1)}, u32[]{:S(2)}, u32[]{:S(2)}) collective-permute-start(bf16[192,1536]{1,0:T(8,128)(2,1)} %collective-permute-done.19), channel_id=1, source_target_pairs={{1,0},{2,1},{5,4},{6,5},{9,8},{10,9},{13,12},{14,13},{17,16},{18,1... | collective-permute-start | bytes 1769480 | tf_op jit(solution)/shard_map/ppermute | solution.py:52
  347.4 21.4 %collective-permute-start.26 = (bf16[384,768]{1,0:T(8,128)(2,1)}, bf16[384,768]{1,0:T(8,128)(2,1)}, u32[]{:S(2)}, u32[]{:S(2)}) collective-permute-start(bf16[384,768]{1,0:T(8,128)(2,1)} %get-tuple-element.488), channel_id=1, source_target_pairs={{0,1},{1,2},{4,5},{5,6},{8,9},{9,10},{12,13},{13,14},{16,17},{17,1... | collective-permute-start | bytes 1769480 | tf_op jit(solution)/shard_map/ppermute | solution.py:100
  401.2 37.4 %all-to-all-start.1 = ((bf16[4,192,384]{2,1,0:T(8,128)(2,1)}), bf16[4,192,384]{2,1,0:T(8,128)(2,1)}, u32[]{:S(2)}, u32[]{:S(2)}) async-start(bf16[4,192,384]{2,1,0:T(8,128)(2,1)} %bitcast.20), calls=%async_computation.1 | async-start | bytes 1179648 | tf_op jit(solution)/shard_map/all_to_all | solution.py:1005
  405.3 175.7 %reduce-scatter.8.cloned.1.call-start = ((), (), s32[]{:S(2)}) async-start(), calls=%async_computation.9 | async-start | bytes 11943936 | tf_op jit(solution)/shard_map/reduce_scatter | solution.py:1020
  407.1 57.5 %collective-permute-start.32 = (bf16[768,192]{0,1:T(8,128)(2,1)}, bf16[768,192]{0,1:T(8,128)(2,1)}, u32[]{:S(2)}, u32[]{:S(2)}) collective-permute-start(bf16[768,192]{0,1:T(8,128)(2,1)} %get-tuple-element.501), channel_id=1, source_target_pairs={{0,1},{4,5},{8,9},{12,13},{16,17},{20,21},{24,25},{28,29}} | collective-permute-start | bytes 884744 | tf_op jit(solution)/shard_map/ppermute | solution.py:100
  411.7 53.0 %collective-permute-start.33 = (bf16[768,192]{0,1:T(8,128)(2,1)}, bf16[768,192]{0,1:T(8,128)(2,1)}, u32[]{:S(2)}, u32[]{:S(2)}) collective-permute-start(bf16[768,192]{0,1:T(8,128)(2,1)} %get-tuple-element.500), channel_id=1, source_target_pairs={{3,2},{7,6},{11,10},{15,14},{19,18},{23,22},{27,26},{31,30}} | collective-permute-start | bytes 884744 | tf_op jit(solution)/shard_map/ppermute | solution.py:101
  440.8 23.8 %collective-permute-start.30 = (bf16[384,768]{1,0:T(8,128)(2,1)S(1)}, bf16[384,768]{1,0:T(8,128)(2,1)}, u32[]{:S(2)}, u32[]{:S(2)}) collective-permute-start(bf16[384,768]{1,0:T(8,128)(2,1)S(1)} %get-tuple-element.478), channel_id=1, source_target_pairs={{0,1},{4,5},{8,9},{12,13},{16,17},{20,21},{24,25},{28,29}} | collective-permute-start | bytes 1769480 | tf_op jit(solution)/shard_map/ppermute | solution.py:100
  442.9 21.7 %collective-permute-start.31 = (bf16[384,768]{1,0:T(8,128)(2,1)S(1)}, bf16[384,768]{1,0:T(8,128)(2,1)}, u32[]{:S(2)}, u32[]{:S(2)}) collective-permute-start(bf16[384,768]{1,0:T(8,128)(2,1)S(1)} %get-tuple-element.477), channel_id=1, source_target_pairs={{3,2},{7,6},{11,10},{15,14},{19,18},{23,22},{27,26},{31,30}} | collective-permute-start | bytes 1769480 | tf_op jit(solution)/shard_map/ppermute | solution.py:101
  464.7 154.9 %reduce-scatter.10.cloned.1.call-start = ((), (), s32[]{:S(2)}) async-start(), calls=%async_computation.10 | async-start | bytes 1327104
  495.0 22.6 %collective-permute-start.42 = (bf16[768,192]{0,1:T(8,128)(2,1)S(1)}, bf16[768,192]{0,1:T(8,128)(2,1)S(1)}, u32[]{:S(2)}, u32[]{:S(2)}) collective-permute-start(bf16[768,192]{0,1:T(8,128)(2,1)S(1)} %get-tuple-element.497), channel_id=1, source_target_pairs={{0,1},{1,2},{2,3},{4,5},{5,6},{6,7},{8,9},{9,10},{10,11},{12,13},{... | collective-permute-start | bytes 884744 | tf_op jit(solution)/shard_map/ppermute | solution.py:100
  502.6 28.8 %collective-permute-start.43 = (bf16[768,192]{0,1:T(8,128)(2,1)}, bf16[768,192]{0,1:T(8,128)(2,1)}, u32[]{:S(2)}, u32[]{:S(2)}) collective-permute-start(bf16[768,192]{0,1:T(8,128)(2,1)} %get-tuple-element.496), channel_id=1, source_target_pairs={{1,0},{2,1},{3,2},{5,4},{6,5},{7,6},{9,8},{10,9},{11,10},{13,12},{... | collective-permute-start | bytes 884744 | tf_op jit(solution)/shard_map/ppermute | solution.py:101
  505.2 26.2 %collective-permute-start.40 = (bf16[384,768]{1,0:T(8,128)(2,1)}, bf16[384,768]{1,0:T(8,128)(2,1)S(1)}, u32[]{:S(2)}, u32[]{:S(2)}) collective-permute-start(bf16[384,768]{1,0:T(8,128)(2,1)} %get-tuple-element.482), channel_id=1, source_target_pairs={{0,1},{1,2},{2,3},{4,5},{5,6},{6,7},{8,9},{9,10},{10,11},{12,13},{... | collective-permute-start | bytes 1769480 | tf_op jit(solution)/shard_map/ppermute | solution.py:100
  510.0 21.5 %collective-permute-start.41 = (bf16[384,768]{1,0:T(8,128)(2,1)}, bf16[384,768]{1,0:T(8,128)(2,1)S(1)}, u32[]{:S(2)}, u32[]{:S(2)}) collective-permute-start(bf16[384,768]{1,0:T(8,128)(2,1)} %get-tuple-element.481), channel_id=1, source_target_pairs={{1,0},{2,1},{3,2},{5,4},{6,5},{7,6},{9,8},{10,9},{11,10},{13,12},{... | collective-permute-start | bytes 1769480 | tf_op jit(solution)/shard_map/ppermute | solution.py:101
  512.2 24.3 %collective-permute-start.38 = (bf16[384,768]{1,0:T(8,128)(2,1)}, bf16[384,768]{1,0:T(8,128)(2,1)}, u32[]{:S(2)}, u32[]{:S(2)}) collective-permute-start(bf16[384,768]{1,0:T(8,128)(2,1)} %get-tuple-element.475), channel_id=1, source_target_pairs={{0,1},{4,5},{8,9},{12,13},{16,17},{20,21},{24,25},{28,29}} | collective-permute-start | bytes 1769480 | tf_op jit(solution)/shard_map/ppermute | solution.py:100
  556.1 20.0 %collective-permute-start.46 = (bf16[384,768]{1,0:T(8,128)(2,1)S(1)}, bf16[384,768]{1,0:T(8,128)(2,1)S(1)}, u32[]{:S(2)}, u32[]{:S(2)}) collective-permute-start(bf16[384,768]{1,0:T(8,128)(2,1)S(1)} %get-tuple-element.472), channel_id=1, source_target_pairs={{0,1},{1,2},{2,3},{4,5},{5,6},{6,7},{8,9},{9,10},{10,11},{12,13},{... | collective-permute-start | bytes 1769480 | tf_op jit(solution)/shard_map/ppermute | solution.py:100
  (119 other events, 1292.3 us)
Sparse Core Ops, SparseCore 0:
  10.5 67.5 all-gather.3
  135.7 70.0 all-gather.5
  344.5 81.1 reduce-scatter.5
  464.8 85.0 reduce-scatter.7
  586.8 32.7 reduce-scatter.9
